TPU v7x, 32 devices: a whole 2x2x4 slice. The times are simulated.
32 devices in a mesh: elem: 8 (over y, x, core), band: 4 (over z).
Axes of the slice: x: 2, y: 2, z: 4, core: 2. Of those that a mesh axis runs over, the one named last changes fastest.
Arguments:
- orbitals: float32 [32, 160, 1024], P('elem', 'band'), may hold values from -6 to 6
- rotation: float32 [1024, 1024], P('band'), may hold values from -0.25 to 0.25
- counts: int32 [32], P('elem'), may hold values from 96 to 160, as said below
- hamiltonian: float32 [32, 7, 160, 160], P('elem'), may hold values from -0.1875 to 0.1875
- filter_center: float32 [1], replicated, may hold values from -0.5 to 0.5
- filter_width: float32 [1], replicated, may hold values from 1.5 to 2.5
Outputs:
- filtered: float32 [32, 160, 1024], P('elem', None, 'band')
Inputs may be any that keep to these rules, and one draw needn't show every extreme that they name: `counts`: some element has exactly 96 and some exactly 160 basis functions.
All inputs are finite; a program needn't handle non-finite values.
Results may differ from a plain program's by a relative error of at most 0.0001.
Values sent between devices are 32-bit elements; how exact they have to be, the bound alone decides.
A program may use at most 64 MiB of HBM per device.

v0:
```python
import jax
import jax.numpy as jnp
from jax import lax
from jax.sharding import PartitionSpec as P

GY = 8


def shifted(shard, axis, by):
    size = lax.axis_size(axis)
    return lax.ppermute(shard, axis, [(i, (i + by) % size) for i in range(size)])


def moved(field, steps):
    return shifted(field, "elem", steps)


def apply_operator(field, hamiltonian, live):
    position = lax.axis_index("elem")
    y_place = position % GY
    z_place = position // GY
    layers = lax.axis_size("elem") // GY
    zero = jnp.float32(0.0)
    y_minus = jnp.where(y_place == 0, moved(field, -(GY - 1)), moved(field, 1))
    y_plus = jnp.where(y_place == GY - 1, moved(field, GY - 1), moved(field, -1))
    z_minus = jnp.where(z_place == 0, zero, moved(field, GY))
    z_plus = jnp.where(z_place == layers - 1, zero, moved(field, -GY))
    others = [
        field,
        jnp.roll(field, 1, axis=0),
        jnp.roll(field, -1, axis=0),
        y_minus,
        y_plus,
        z_minus,
        z_plus,
    ]
    total = jnp.zeros(field.shape, jnp.float32)
    for slot in range(7):
        total = total + jnp.einsum(
            "erc,ecb->erb", hamiltonian[:, slot], others[slot], precision=lax.Precision.HIGHEST
        )
    return jnp.where(live[:, :, None], total, zero)


def shards(orbitals, rotation, counts, hamiltonian, filter_center, filter_width):
    elements, rows_here, bands = orbitals.shape
    basis = hamiltonian.shape[2]
    row_index = lax.axis_index("band") * rows_here + jnp.arange(rows_here, dtype=jnp.int32)
    masked = jnp.where(
        (row_index[None, :] < counts[:, None])[:, :, None], orbitals, jnp.float32(0.0)
    )
    by_columns = lax.all_to_all(masked, "band", split_axis=2, concat_axis=1, tiled=True)
    flat_rows = by_columns.reshape(elements * basis, by_columns.shape[2])
    summed = lax.psum_scatter(
        jnp.einsum("kb,mk->bm", rotation, flat_rows, precision=lax.Precision.HIGHEST),
        "band",
        scatter_dimension=0,
        tiled=True,
    )
    start = jnp.transpose(summed.reshape(summed.shape[0], elements, basis), (1, 2, 0))
    live = jnp.arange(basis, dtype=jnp.int32)[None, :] < counts[:, None]
    center = filter_center[0]
    width = filter_width[0]
    middle = (apply_operator(start, hamiltonian, live) - center * start) / width
    filtered = 2.0 * (apply_operator(middle, hamiltonian, live) - center * middle) / width - start
    return filtered


def solution(mesh):
    return jax.shard_map(
        shards,
        mesh=mesh,
        in_specs=(
            P("elem", "band", None),
            P("band", None),
            P("elem"),
            P("elem", None, None, None),
            P(),
            P(),
        ),
        out_specs=P("elem", None, "band"),
        check_vma=False,
    )
```

profile of v0, /device:TPU:0, one launch (start us, length us, event | category | flops | bytes accessed | tf_op | source)
XLA Modules:
  0.0 152.6 jit_solution(3571634080136244972)
XLA Ops:
  6.5 0.8 broadcast_compare_fusion
  7.4 2.0 %broadcast_select_fusion = f32[4,40,1024]{2,1,0:T(8,128)} fusion(f32[4,40,1024]{2,1,0:T(8,128)} %param.6, pred[4,40]{1,0:T(4,128)(4,1)S(1)} %broadcast_compare_fusion), kind=kLoop, calls=%fused_computation.79 | loop fusion | flops 163840 | bytes 1310880 | tf_op jit(solution)/shard_map/jit(_where)/select_n | solution.py:49
  9.4 1.8 %copy.41 = f32[4,40,1024]{1,0,2:T(4,128)S(1)} copy(f32[4,40,1024]{2,1,0:T(8,128)} %broadcast_select_fusion) | data formatting | bytes 1310720 | tf_op jit(solution)/shard_map/jit(_where)/select_n | solution.py:49
  11.2 3.7 %reshape.60 = f32[4,1,40960]{2,1,0:T(1,128)} reshape(f32[1024,4,40]{2,1,0:T(4,128)S(1)} %bitcast.101) | data formatting | bytes 1310720
  14.9 23.6 %all_to_all.15 = f32[4,1,40960]{2,1,0:T(1,128)S(1)} all-to-all(f32[4,1,40960]{2,1,0:T(1,128)} %reshape.60), channel_id=1, replica_groups=mesh['elem'=8,'band'=4] {'band'}, dimensions={0} | all-to-all | bytes 1310720 | tf_op jit(solution)/shard_map/all_to_all | solution.py:52
  39.1 3.3 %reduce = f32[4,40960]{1,0:T(4,128)} reduce(f32[4,1,40960]{2,1,0:T(1,128)S(1)} %all_to_all.15, f32[]{:T(128)} %broadcast.47), dimensions={1}, to_apply=%all_to_all.11.reduce_sub_computation | reduce | bytes 1310724 | tf_op jit(solution)/shard_map/all_to_all | solution.py:52
  42.4 4.2 %reshape.61 = f32[1024,4,40]{2,1,0:T(4,128)S(1)} reshape(f32[4,40960]{1,0:T(4,128)} %reduce) | data formatting | bytes 1310720
  46.6 1.5 copy.43
  48.2 4.9 %convolution_bitcast_fusion = f32[1024,640]{0,1:T(8,128)} fusion(f32[640,256]{1,0:T(8,128)} %bitcast.103, f32[256,1024]{1,0:T(8,128)S(1)} %copy-done), kind=kOutput, calls=%fused_computation | convolution fusion | flops 2013265920 | bytes 4325376 | tf_op jit(solution)/shard_map/kb,mk->bm/dot_general | solution.py:55
  54.5 49.9 %reduce-scatter.2.cloned.1.call-done = f32[256,640]{0,1:T(8,128)} async-done(((f32[1024,640]{0,1:T(8,128)}), f32[256,640]{0,1:T(8,128)}) %reduce-scatter.2.cloned.1.call-update) | async-done | bytes 655376 | tf_op jit(solution)/shard_map/reduce_scatter | solution.py:54
  104.4 1.1 collective-permute-start.2
  105.5 1.2 fusion.86
  106.8 1.7 %collective-permute-start.1 = (f32[4,160,256]{2,1,0:T(8,128)}, f32[4,160,256]{2,1,0:T(8,128)S(1)}, u32[]{:S(2)}, u32[]{:S(2)}) collective-permute-start(f32[4,160,256]{2,1,0:T(8,128)} %bitcast.95), channel_id=1, source_target_pairs={{0,28},{4,0},{8,4},{12,8},{16,12},{20,16},{24,20},{28,24},{1,29},{... | collective-permute-start | bytes 1966088 | tf_op jit(solution)/shard_map/ppermute | solution.py:11
  108.5 2.0 %fusion.48 = f32[4,256,160]{1,2,0:T(8,128)S(1)} fusion(f32[4,160,256]{2,1,0:T(8,128)} %bitcast.97, f32[4,7,160,160]{3,2,1,0:T(8,128)} %param.9), kind=kOutput, calls=%fused_computation.55 | convolution fusion | flops 314572800 | bytes 1966080 | tf_op jit(solution)/shard_map/erc,ecb->erb/dot_general | solution.py:39
  110.6 1.0 fusion.87
  111.6 1.9 %convolution_add_fusion.5 = f32[4,256,160]{1,2,0:T(8,128)S(1)} fusion(f32[4,256,160]{1,2,0:T(8,128)S(1)} %fusion.48, f32[3,160,256]{2,1,0:T(8,128)S(1)} %get-tuple-element.10, f32[1,160,256]{2,1,0:T(8,128)S(1)} %get-tuple-element.12, f32[4,7,160,160]{3,2,1,0:T(8,128)} %param.9), kind=kOutput, calls=%fused_computation.22 | convolution fusion | flops 314900480 | bytes 2621440 | tf_op jit(solution)/shard_map/erc,ecb->erb/dot_general | solution.py:39
  113.5 1.9 %convolution_add_fusion.4 = f32[4,256,160]{1,2,0:T(8,128)S(1)} fusion(f32[4,256,160]{1,2,0:T(8,128)S(1)} %convolution_add_fusion.5, f32[1,160,256]{2,1,0:T(8,128)S(1)} %get-tuple-element.11, f32[3,160,256]{2,1,0:T(8,128)S(1)} %get-tuple-element.9, f32[4,7,160,160]{3,2,1,0:T(8,128)} %param.9), kind=kOutput, calls=%fused_computation.21 | convolution fusion | flops 314900480 | bytes 2621440 | tf_op jit(solution)/shard_map/erc,ecb->erb/dot_general | solution.py:39
  117.0 6.4 %collective-permute-done.1 = f32[4,160,256]{2,1,0:T(8,128)S(1)} collective-permute-done((f32[4,160,256]{2,1,0:T(8,128)}, f32[4,160,256]{2,1,0:T(8,128)S(1)}, u32[]{:S(2)}, u32[]{:S(2)}) %collective-permute-start.1) | collective-permute-done | bytes 655392 | tf_op jit(solution)/shard_map/ppermute | solution.py:11
  124.2 0.8 collective-permute-done
  125.0 1.0 fusion.15
  126.9 2.0 %collective-permute-start.4 = (f32[4,160,256]{2,1,0:T(8,128)S(1)}, f32[4,160,256]{2,1,0:T(8,128)S(1)}, u32[]{:S(2)}, u32[]{:S(2)}) collective-permute-start(f32[4,160,256]{2,1,0:T(8,128)S(1)} %fusion.15), channel_id=1, source_target_pairs={{0,28},{4,0},{8,4},{12,8},{16,12},{20,16},{24,20},{28,24},{1,29},{... | collective-permute-start | bytes 1966088 | tf_op jit(solution)/shard_map/ppermute | solution.py:11
  132.1 9.9 %collective-permute-done.4 = f32[4,160,256]{2,1,0:T(8,128)S(1)} collective-permute-done((f32[4,160,256]{2,1,0:T(8,128)S(1)}, f32[4,160,256]{2,1,0:T(8,128)S(1)}, u32[]{:S(2)}, u32[]{:S(2)}) %collective-permute-start.4) | collective-permute-done | bytes 655392 | tf_op jit(solution)/shard_map/ppermute | solution.py:11
  142.7 1.1 collective-permute-done.3
  143.9 1.9 %fusion.8 = f32[4,160,256]{2,1,0:T(8,128)} fusion(f32[4,160,256]{2,1,0:T(8,128)S(1)} %bitcast.100, f32[4,256,160]{1,2,0:T(8,128)S(1)} %fusion.28, f32[4,256,160]{1,2,0:T(8,128)S(1)} %fusion.32, f32[4,256,160]{1,2,0:T(8,128)S(1)} %fusion.36, f32[4,256,160]{1,2,0:T(8,128)S(1)} %convolution_add_fusion.1, f32[4,160,256]{2,1,0:T(8,128)S(1)} %collective-permute-done.3, ...), kind=kOutput, calls=%fused_computation.10 | convolution fusion | flops 316211200 | bytes 5899272 | tf_op jit(solution)/shard_map/erc,ecb->erb/dot_general | solution.py:39
  (32 shorter events, 7.9 us)
Async XLA Ops:
  6.5 41.6 %copy-start = (f32[256,1024]{1,0:T(8,128)S(1)}, f32[256,1024]{1,0:T(8,128)}, u32[]{:S(2)}) copy-start(f32[256,1024]{1,0:T(8,128)} %param.7) | copy-start | bytes 3145732
  6.5 97.9 %reduce-scatter.2.cloned.1.call-start = ((), (), s32[]{:S(2)}) async-start(), calls=%async_computation.2 | async-start | bytes 3276800 | tf_op jit(solution)/shard_map/reduce_scatter | solution.py:54
  46.6 7.8 %copy-start.2 = (s32[4]{0:T(128)S(1)}, s32[4]{0:T(128)}, u32[]{:S(2)}) copy-start(s32[4]{0:T(128)} %param.8) | copy-start | bytes 52
  53.0 62.4 %slice-start = ((s8[4587520]{0:T(1024)(128)(4,1)}), s8[393216]{0:T(1024)(128)(4,1)S(1)}, s32[]{:S(2)}) async-start(s8[4587520]{0:T(1024)(128)(4,1)} %bitcast.91), calls=%async_computation.3 | async-start | bytes 786432
  104.4 11.0 %collective-permute-start.2 = (f32[4,160,256]{2,1,0:T(8,128)}, f32[4,160,256]{2,1,0:T(8,128)S(1)}, u32[]{:S(2)}, u32[]{:S(2)}) collective-permute-start(f32[4,160,256]{2,1,0:T(8,128)} %bitcast.93), channel_id=1, source_target_pairs={{0,0},{4,4},{8,8},{12,12},{16,16},{20,20},{24,24},{28,28},{1,1},{5... | collective-permute-start | bytes 1966088 | tf_op jit(solution)/shard_map/ppermute | solution.py:11
  106.8 8.7 %slice-start.1 = ((s8[4587520]{0:T(1024)(128)(4,1)}), s8[4194304]{0:T(1024)(128)(4,1)S(1)}, s32[]{:S(2)}) async-start(s8[4587520]{0:T(1024)(128)(4,1)} %bitcast.91), calls=%async_computation.4 | async-start | bytes 8388608
  106.8 16.7 %collective-permute-start.1 = (f32[4,160,256]{2,1,0:T(8,128)}, f32[4,160,256]{2,1,0:T(8,128)S(1)}, u32[]{:S(2)}, u32[]{:S(2)}) collective-permute-start(f32[4,160,256]{2,1,0:T(8,128)} %bitcast.95), channel_id=1, source_target_pairs={{0,28},{4,0},{8,4},{12,8},{16,12},{20,16},{24,20},{28,24},{1,29},{... | collective-permute-start | bytes 1966088 | tf_op jit(solution)/shard_map/ppermute | solution.py:11
  108.5 16.5 %collective-permute-start = (f32[4,160,256]{2,1,0:T(8,128)}, f32[4,160,256]{2,1,0:T(8,128)S(1)}, u32[]{:S(2)}, u32[]{:S(2)}) collective-permute-start(f32[4,160,256]{2,1,0:T(8,128)} %bitcast.96), channel_id=1, source_target_pairs={{0,4},{4,8},{8,12},{12,16},{16,20},{20,24},{24,28},{28,0},{1,5},{5... | collective-permute-start | bytes 1966088 | tf_op jit(solution)/shard_map/ppermute | solution.py:11
  113.4 11.6 %copy-start.1 = (f32[256,640]{0,1:T(8,128)S(1)}, f32[256,640]{0,1:T(8,128)}, u32[]{:S(2)}) copy-start(f32[256,640]{0,1:T(8,128)} %reduce-scatter.2.cloned.1.call-done) | copy-start | bytes 1966084
  126.9 3.6 %collective-permute-start.5 = (f32[4,160,256]{2,1,0:T(8,128)S(1)}, f32[4,160,256]{2,1,0:T(8,128)S(1)}, u32[]{:S(2)}, u32[]{:S(2)}) collective-permute-start(f32[4,160,256]{2,1,0:T(8,128)S(1)} %fusion.15), channel_id=1, source_target_pairs={{0,0},{4,4},{8,8},{12,12},{16,16},{20,20},{24,24},{28,28},{1,1},{5... | collective-permute-start | bytes 1966088 | tf_op jit(solution)/shard_map/ppermute | solution.py:11
  126.9 15.0 %collective-permute-start.4 = (f32[4,160,256]{2,1,0:T(8,128)S(1)}, f32[4,160,256]{2,1,0:T(8,128)S(1)}, u32[]{:S(2)}, u32[]{:S(2)}) collective-permute-start(f32[4,160,256]{2,1,0:T(8,128)S(1)} %fusion.15), channel_id=1, source_target_pairs={{0,28},{4,0},{8,4},{12,8},{16,12},{20,16},{24,20},{28,24},{1,29},{... | collective-permute-start | bytes 1966088 | tf_op jit(solution)/shard_map/ppermute | solution.py:11
  128.9 14.9 %collective-permute-start.3 = (f32[4,160,256]{2,1,0:T(8,128)S(1)}, f32[4,160,256]{2,1,0:T(8,128)S(1)}, u32[]{:S(2)}, u32[]{:S(2)}) collective-permute-start(f32[4,160,256]{2,1,0:T(8,128)S(1)} %fusion.15), channel_id=1, source_target_pairs={{0,4},{4,8},{8,12},{12,16},{16,20},{20,24},{24,28},{28,0},{1,5},{5... | collective-permute-start | bytes 1966088 | tf_op jit(solution)/shard_map/ppermute | solution.py:11
Sparse Core Ops, SparseCore 0:
  53.2 51.2 reduce-scatter.1
where the time goes:
time: 153 us
  waiting for transfers between devices  68.1 us (45%)
  blocking collectives  23.6 us (15%)
  matrix products  20.6 us (13%)
  between operations  15 us (10%)
  local copies, waits for them, and re-layouts  14.2 us (9%)
  other arithmetic  6.27 us (4%)
  starting transfers between devices  4.84 us (3%)
    reduce_scatter x1, waiting for transfers between devices, shards(): lax.psum_scatter(jnp.einsum('kb,mk->bm', rotation, flat_rows, precision=l...  49.9 us
    all_to_all x1, blocking collectives, shards(): lax.all_to_all(masked, 'band', split_axis=2, concat_axis=1, tiled=True)  23.6 us
    ppermute x6, waiting for transfers between devices, shifted(): lax.ppermute(shard, axis, [(i, (i + by) % size) for i in range(size)])  18.2 us
    dot_general x14, matrix products, apply_operator(): jnp.einsum('erc,ecb->erb', hamiltonian[:, slot], others[slot], precision=...  15.7 us
    unnamed x12, local copies, waits for them, and re-layouts  7.98 us
    dot_general x1, matrix products, shards(): jnp.einsum('kb,mk->bm', rotation, flat_rows, precision=lax.Precision.HIGH...  4.86 us
    ppermute x6, starting transfers between devices, shifted(): lax.ppermute(shard, axis, [(i, (i + by) % size) for i in range(size)])  4.84 us
    all_to_all x1, other arithmetic, shards(): lax.all_to_all(masked, 'band', split_axis=2, concat_axis=1, tiled=True)  3.34 us
  transfers between devices with their start and end apart: 7, of which 5 were waited for; matrix products, arithmetic and copies ran while one was open for 9% of the time, Pallas kernels for 0%

commit v1 on v0

v1 whole, which is shorter than its diff:
```python
import jax
import jax.numpy as jnp
from jax import lax
from jax.sharding import PartitionSpec as P

GY = 8


def neighbour_rows(field, stride, span, wraps):
    size = lax.axis_size("elem")
    behind, ahead = [], []
    for i in range(size):
        place = (i // stride) % span
        base = i - place * stride
        if wraps or place + 1 < span:
            behind.append((i, base + (place + 1) % span * stride))
        if wraps or place > 0:
            ahead.append((i, base + (place + span - 1) % span * stride))
    return lax.ppermute(field, "elem", behind), lax.ppermute(field, "elem", ahead)


def apply_operator(field, hamiltonian, live):
    layers = lax.axis_size("elem") // GY
    others = [field, jnp.roll(field, 1, axis=0), jnp.roll(field, -1, axis=0)]
    others += neighbour_rows(field, 1, GY, True)
    if layers > 1:
        others += neighbour_rows(field, GY, layers, False)
    total = jnp.zeros(field.shape, jnp.float32)
    for slot, other in enumerate(others):
        total = total + jnp.einsum(
            "erc,ecb->erb", hamiltonian[:, slot], other, precision=lax.Precision.HIGH
        )
    return jnp.where(live[:, :, None], total, jnp.float32(0.0))


def shards(orbitals, rotation, counts, hamiltonian, filter_center, filter_width):
    elements, rows_here, bands = orbitals.shape
    basis = hamiltonian.shape[2]
    whole_rotation = lax.all_gather(rotation, "band", axis=0, tiled=True)
    rotated = jnp.einsum(
        "eik,kb->eib", orbitals, whole_rotation, precision=lax.Precision.HIGH
    )
    start = lax.all_to_all(rotated, "band", split_axis=2, concat_axis=1, tiled=True)
    live = jnp.arange(basis, dtype=jnp.int32)[None, :] < counts[:, None]
    start = jnp.where(live[:, :, None], start, jnp.float32(0.0))
    center = filter_center[0]
    width = filter_width[0]
    middle = (apply_operator(start, hamiltonian, live) - center * start) / width
    return 2.0 * (apply_operator(middle, hamiltonian, live) - center * middle) / width - start


def solution(mesh):
    return jax.shard_map(
        shards,
        mesh=mesh,
        in_specs=(
            P("elem", "band", None),
            P("band", None),
            P("elem"),
            P("elem", None, None, None),
            P(),
            P(),
        ),
        out_specs=P("elem", None, "band"),
        check_vma=False,
    )
```

time: 153 us -> 177 us (1.16)
  waiting for transfers between devices: 68.1 us -> 128 us
  blocking collectives: 23.6 us -> 0 us
  matrix products: 20.6 us -> 11.4 us
  local copies, waits for them, and re-layouts: 14.2 us -> 11.1 us
    all_gather x0 -> x1, waiting for transfers between devices: none -> 85.2 us  [shards(): whole_rotation = lax.all_gather(rotation, 'band', axis=0, tiled=True)]
    reduce_scatter x1 -> x0, waiting for transfers between devices: 49.9 us -> none  [shards(): lax.psum_scatter(jnp.einsum('kb,mk->bm', rotation, flat_rows, precision=l...]
    all_to_all x1 -> x0, blocking collectives: 23.6 us -> none  [shards(): lax.all_to_all(masked, 'band', split_axis=2, concat_axis=1, tiled=True)]
    all_to_all x0 -> x1, waiting for transfers between devices: none -> 16.2 us  [shards(): lax.all_to_all(rotated, 'band', split_axis=2, concat_axis=1, tiled=True)]
    dot_general x15 -> x11, matrix products: 20.6 us -> 11.4 us  [the longest x10 7.76 us: apply_operator(): jnp.einsum('erc,ecb->erb', hamiltonian[:, slot], other, precision=lax.Pre...]
    ppermute x6 -> x4, waiting for transfers between devices: 18.2 us -> 25.8 us  [the longest x2 24.2 us: neighbour_rows(): lax.ppermute(field, 'elem', ahead)]
    all_to_all x0 -> x1, starting transfers between devices: none -> 3.48 us  [shards(): lax.all_to_all(rotated, 'band', split_axis=2, concat_axis=1, tiled=True)]
    slice x4, local copies, waits for them, and re-layouts: 2.36 us -> 0.21 us  [apply_operator(): others = [field, jnp.roll(field, 1, axis=0), jnp.roll(field, -1, axis=0)]]
  transfers between devices with their start and end apart: 7 -> 6, of which waited for: 5 -> 6; matrix products, arithmetic and copies ran while one was open for 9% -> 3% of each run, Pallas kernels for 0% -> 0%
where the time goes in v1:
time: 177 us; the launch traced here: 176 us
  waiting for transfers between devices  128 us (72%)
  between operations  14.9 us (8%)
  matrix products  11.4 us (6%)
  local copies, waits for them, and re-layouts  11.1 us (6%)
  starting transfers between devices  6.25 us (4%)
  other arithmetic  4.91 us (3%)
    all_gather x1, waiting for transfers between devices, shards(): whole_rotation = lax.all_gather(rotation, 'band', axis=0, tiled=True)  85.2 us
    ppermute x2, waiting for transfers between devices, neighbour_rows(): lax.ppermute(field, 'elem', ahead)  24.2 us
    all_to_all x1, waiting for transfers between devices, shards(): lax.all_to_all(rotated, 'band', split_axis=2, concat_axis=1, tiled=True)  16.2 us
    unnamed x10, local copies, waits for them, and re-layouts  7.97 us
    dot_general x10, matrix products, apply_operator(): jnp.einsum('erc,ecb->erb', hamiltonian[:, slot], other, precision=lax.Pre...  7.76 us
    dot_general x1, matrix products, shards(): jnp.einsum('eik,kb->eib', orbitals, whole_rotation, precision=lax.Precisi...  3.63 us
  transfers between devices with their start and end apart: 6, of which 6 were waited for; matrix products, arithmetic and copies ran while one was open for 3% of the time, Pallas kernels for 0%

profile of v1, /device:TPU:0, one launch (start us, length us, event | category | flops | bytes accessed | tf_op | source)
XLA Modules:
  0.0 176.5 jit_solution(5742808455843046785)
XLA Ops:
  6.5 0.7 all-gather.2.cloned.1.call-update
  7.3 85.2 %all-gather.2.cloned.1.call-done = f32[1024,1024]{1,0:T(8,128)} async-done(((f32[256,1024]{1,0:T(8,128)}), f32[1024,1024]{1,0:T(8,128)}) %all-gather.2.cloned.1.call-update) | async-done | bytes 4194320 | tf_op jit(solution)/shard_map/all_gather | solution.py:39
  92.4 3.6 %fusion = f32[4,40,1024]{2,1,0:T(8,128)S(1)} fusion(f32[4,40,1024]{2,1,0:T(8,128)S(1)} %copy-done, f32[1024,1024]{1,0:T(8,128)} %all-gather.2.cloned.1.call-done), kind=kOutput, calls=%fused_computation | convolution fusion | flops 1006632960 | bytes 5505024 | tf_op jit(solution)/shard_map/eik,kb->eib/dot_general | solution.py:40
  96.1 0.9 copy.13
  97.0 3.7 %reshape.22 = f32[4,1,40960]{2,1,0:T(1,128)} reshape(f32[1024,4,40]{2,1,0:T(4,128)S(1)} %bitcast.76) | data formatting | bytes 1310720
  100.7 3.5 %all-to-all-start = ((f32[4,1,40960]{2,1,0:T(1,128)}), f32[4,1,40960]{2,1,0:T(1,128)S(1)}, u32[]{:S(2)}, u32[]{:S(2)}) async-start(f32[4,1,40960]{2,1,0:T(1,128)} %reshape.22), calls=%async_computation | async-start | bytes 1310720 | tf_op jit(solution)/shard_map/all_to_all | solution.py:43
  105.6 16.2 %all-to-all-done = f32[4,1,40960]{2,1,0:T(1,128)S(1)} async-done(((f32[4,1,40960]{2,1,0:T(1,128)}), f32[4,1,40960]{2,1,0:T(1,128)S(1)}, u32[]{:S(2)}, u32[]{:S(2)}) %all-to-all-start) | async-done | bytes 655392 | tf_op jit(solution)/shard_map/all_to_all | solution.py:43
  121.7 0.6 broadcast.23
  122.3 3.4 %reduce = f32[4,40960]{1,0:T(4,128)} reduce(f32[4,1,40960]{2,1,0:T(1,128)S(1)} %all-to-all-done, f32[]{:T(128)} %broadcast.23), dimensions={1}, to_apply=%all_to_all.13.reduce_sub_computation | reduce | bytes 1310724 | tf_op jit(solution)/shard_map/all_to_all | solution.py:43
  125.8 4.2 %reshape.23 = f32[1024,4,40]{2,1,0:T(4,128)S(1)} reshape(f32[4,40960]{1,0:T(4,128)} %reduce) | data formatting | bytes 1310720
  130.0 1.5 copy.14
  131.5 1.4 bitcast_select_fusion
  132.9 1.1 collective-permute-start.1
  134.2 1.5 fusion.38
  135.8 1.5 convolution_add_fusion.5
  137.3 0.4 convolution_add_fusion.4
  137.8 11.4 %collective-permute-done.1 = f32[4,160,256]{2,1,0:T(8,128)S(1)} collective-permute-done((f32[4,160,256]{2,1,0:T(8,128)S(1)}, f32[4,160,256]{2,1,0:T(8,128)S(1)}, u32[]{:S(2)}, u32[]{:S(2)}) %collective-permute-start.1) | collective-permute-done | bytes 655392 | tf_op jit(solution)/shard_map/ppermute | solution.py:19
  149.6 1.3 collective-permute-done
  150.9 0.6 fusion.13
  151.5 1.5 collective-permute-start.3
  154.1 0.5 convolution_add_fusion.1
  154.6 12.8 %collective-permute-done.3 = f32[4,160,256]{2,1,0:T(8,128)S(1)} collective-permute-done((f32[4,160,256]{2,1,0:T(8,128)S(1)}, f32[4,160,256]{2,1,0:T(8,128)S(1)}, u32[]{:S(2)}, u32[]{:S(2)}) %collective-permute-start.3) | collective-permute-done | bytes 655392 | tf_op jit(solution)/shard_map/ppermute | solution.py:19
  167.4 0.4 fusion.26
  168.1 1.5 fusion.8
  (21 shorter events, 2.0 us)
Async XLA Ops:
  6.5 85.9 %copy-start = (f32[4,40,1024]{2,1,0:T(8,128)S(1)}, f32[4,40,1024]{2,1,0:T(8,128)}, u32[]{:S(2)}) copy-start(f32[4,40,1024]{2,1,0:T(8,128)} %param.6) | copy-start | bytes 1966084
  6.5 85.9 %all-gather.2.cloned.1.call-start = ((), (), s32[]{:S(2)}) async-start(), calls=%async_computation.1 | async-start | bytes 5242880 | tf_op jit(solution)/shard_map/all_gather | solution.py:39
  96.1 9.4 %copy-start.1 = (s32[4]{0:T(128)S(1)}, s32[4]{0:T(128)}, u32[]{:S(2)}) copy-start(s32[4]{0:T(128)} %param.8) | copy-start | bytes 52
  100.7 21.0 %all-to-all-start = ((f32[4,1,40960]{2,1,0:T(1,128)}), f32[4,1,40960]{2,1,0:T(1,128)S(1)}, u32[]{:S(2)}, u32[]{:S(2)}) async-start(f32[4,1,40960]{2,1,0:T(1,128)} %reshape.22), calls=%async_computation | async-start | bytes 1310720 | tf_op jit(solution)/shard_map/all_to_all | solution.py:43
  122.3 15.0 %slice-start = ((s8[4587520]{0:T(1024)(128)(4,1)}), s8[393216]{0:T(1024)(128)(4,1)S(1)}, s32[]{:S(2)}) async-start(s8[4587520]{0:T(1024)(128)(4,1)} %bitcast.74), calls=%async_computation.2 | async-start | bytes 786432
  131.5 5.8 %slice-start.1 = ((s8[4587520]{0:T(1024)(128)(4,1)}), s8[4194304]{0:T(1024)(128)(4,1)S(1)}, s32[]{:S(2)}) async-start(s8[4587520]{0:T(1024)(128)(4,1)} %bitcast.74), calls=%async_computation.3 | async-start | bytes 8388608
  132.9 16.3 %collective-permute-start.1 = (f32[4,160,256]{2,1,0:T(8,128)S(1)}, f32[4,160,256]{2,1,0:T(8,128)S(1)}, u32[]{:S(2)}, u32[]{:S(2)}) collective-permute-start(f32[4,160,256]{2,1,0:T(8,128)S(1)} %bitcast_select_fusion), channel_id=1, source_target_pairs={{0,28},{4,0},{8,4},{12,8},{16,12},{20,16},{24,20},{28,24},{1,29},{... | collective-permute-start | bytes 1966088 | tf_op jit(solution)/shard_map/ppermute | solution.py:19
  134.1 16.8 %collective-permute-start = (f32[4,160,256]{2,1,0:T(8,128)S(1)}, f32[4,160,256]{2,1,0:T(8,128)S(1)}, u32[]{:S(2)}, u32[]{:S(2)}) collective-permute-start(f32[4,160,256]{2,1,0:T(8,128)S(1)} %bitcast_select_fusion), channel_id=1, source_target_pairs={{0,4},{4,8},{8,12},{12,16},{16,20},{20,24},{24,28},{28,0},{1,5},{5... | collective-permute-start | bytes 1966088 | tf_op jit(solution)/shard_map/ppermute | solution.py:19
  151.5 15.9 %collective-permute-start.3 = (f32[4,160,256]{2,1,0:T(8,128)S(1)}, f32[4,160,256]{2,1,0:T(8,128)S(1)}, u32[]{:S(2)}, u32[]{:S(2)}) collective-permute-start(f32[4,160,256]{2,1,0:T(8,128)S(1)} %fusion.13), channel_id=1, source_target_pairs={{0,28},{4,0},{8,4},{12,8},{16,12},{20,16},{24,20},{28,24},{1,29},{... | collective-permute-start | bytes 1966088 | tf_op jit(solution)/shard_map/ppermute | solution.py:19
  153.6 14.5 %collective-permute-start.2 = (f32[4,160,256]{2,1,0:T(8,128)S(1)}, f32[4,160,256]{2,1,0:T(8,128)S(1)}, u32[]{:S(2)}, u32[]{:S(2)}) collective-permute-start(f32[4,160,256]{2,1,0:T(8,128)S(1)} %fusion.13), channel_id=1, source_target_pairs={{0,4},{4,8},{8,12},{12,16},{16,20},{20,24},{24,28},{28,0},{1,5},{5... | collective-permute-start | bytes 1966088 | tf_op jit(solution)/shard_map/ppermute | solution.py:19
Sparse Core Ops, SparseCore 0:
  8.9 83.4 all-gather.1

commit v2 on v1

--- a/solution.py
+++ b/solution.py
@@ -1,6 +1,10 @@
+import functools
+
 import jax
 import jax.numpy as jnp
 from jax import lax
+from jax.experimental import pallas as pl
+from jax.experimental.pallas import tpu as pltpu
 from jax.sharding import PartitionSpec as P
 
 GY = 8
@@ -33,7 +37,7 @@
     return jnp.where(live[:, :, None], total, jnp.float32(0.0))
 
 
-def shards(orbitals, rotation, counts, hamiltonian, filter_center, filter_width):
+def general_shards(orbitals, rotation, counts, hamiltonian, filter_center, filter_width):
     elements, rows_here, bands = orbitals.shape
     basis = hamiltonian.shape[2]
     whole_rotation = lax.all_gather(rotation, "band", axis=0, tiled=True)
@@ -49,9 +53,328 @@
     return 2.0 * (apply_operator(middle, hamiltonian, live) - center * middle) / width - start
 
 
+F32, BF16 = jnp.float32, jnp.bfloat16
+PARTS = 2
+SLOTS = 5
+
+
+def split(x):
+    high = x.astype(BF16)
+    return high, (x - high.astype(F32)).astype(BF16)
+
+
+def kernel(
+    n, orb, rot, counts, center, width, ham, out,
+    ham_v, ham_b, orb_b, rot_b, res, acc_r, start, start_lo, start_hi, mid, mid_lo, mid_hi,
+    field, acc, ham_sem,
+    up_s, dn_s, z_r, y_s, y_r, c_s, c_r, a_s, a_r, h_s, h_r,
+):
+    e, z = lax.axis_index("elem"), lax.axis_index("band")
+    elements, basis = ham.shape[0], ham.shape[2]
+    rows = basis // n
+    depth = rot.shape[0]
+    lanes = start.shape[3]
+    share = depth // 4
+    y, c = e // 4, e % 2
+    ahead, behind = lax.rem(e + 1, 8), lax.rem(e + 7, 8)
+    across, twin = lax.rem(e + 4, 8), e + 1 - 2 * c
+    others = [lax.rem(z + j, n) for j in range(1, n)]
+
+    def remote(src, dst, send, recv, elem, band):
+        return pltpu.make_async_remote_copy(
+            src_ref=src, dst_ref=dst, send_sem=send, recv_sem=recv,
+            device_id=(elem, band), device_id_type=pl.DeviceIdType.MESH,
+        )
+
+    def block(ref, part, s, yy, cc):
+        first = pl.multiple_of((yy * 2 + cc) * share, share)
+        return ref.at[part, s, pl.ds(first, share)]
+
+    def up(part, s):
+        b = block(rot_b, part, s, y, c)
+        return remote(b, b, up_s.at[part, s], z_r.at[part, s], e, z + 1)
+
+    def down(part, s):
+        b = block(rot_b, part, s, y, c)
+        return remote(b, b, dn_s.at[part, s], z_r.at[part, s], e, z - 1)
+
+    def over_y(part, s):
+        b = block(rot_b, part, s, y, c)
+        return remote(b, b, y_s.at[part, s], y_r.at[part, s], across, z)
+
+    def over_core(part, s, far):
+        yy = 1 - y if far else y
+        b = block(rot_b, part, s, yy, c)
+        return remote(b, b, c_s.at[part, s, far], c_r.at[part, s, far], twin, z)
+
+    def got(dst, recv):
+        remote(dst, dst, recv, recv, twin, z).wait_recv()
+
+    def to_band(part, to):
+        return remote(
+            res.at[part, to],
+            start.at[part, :, pl.ds(pl.multiple_of(z * rows, rows), rows)],
+            a_s.at[part, to], a_r.at[part, z], e, to,
+        )
+
+    def rows_of(ref, part, s):
+        return ref.at[part, :, pl.ds(pl.multiple_of(s * rows, rows), rows)]
+
+    def halo(stage, part, s):
+        own, lo, hi = ((start, start_lo, start_hi), (mid, mid_lo, mid_hi))[stage]
+        b = rows_of(own, part, s)
+        return (
+            remote(b, rows_of(lo, part, s), h_s.at[stage, part, s, 0], h_r.at[stage, part, s, 0], ahead, z),
+            remote(b, rows_of(hi, part, s), h_s.at[stage, part, s, 1], h_r.at[stage, part, s, 1], behind, z),
+        )
+
+    barrier = pltpu.get_barrier_semaphore()
+    partners = [(ahead, z), (behind, z), (across, z)] + [(e, other) for other in others]
+    for elem, band in partners:
+        pl.semaphore_signal(barrier, inc=1, device_id=(elem, band), device_id_type=pl.DeviceIdType.MESH)
+    ham_copy = pltpu.make_async_copy(ham.at[:, pl.ds(0, SLOTS)], ham_v, ham_sem)
+    ham_copy.start()
+    for part in range(PARTS):
+        for b in range(n):
+            rot_b[part, z, :, b * lanes:(b + 1) * lanes] = rot[:, (b * PARTS + part) * lanes:(b * PARTS + part + 1) * lanes]
+    pl.semaphore_wait(barrier, len(partners))
+
+    def send_own(part):
+        @pl.when(z < n - 1)
+        def _():
+            up(part, z).start()
+
+        @pl.when(z > 0)
+        def _():
+            down(part, z).start()
+
+    def relay(part, d):
+        @pl.when(z >= d)
+        def _():
+            s = z - d
+            got(block(rot_b, part, s, y, c), z_r.at[part, s])
+
+            @pl.when(z < n - 1)
+            def _():
+                up(part, s).start()
+
+            over_y(part, s).start()
+            over_core(part, s, 0).start()
+
+        @pl.when(z + d < n)
+        def _():
+            s = z + d
+            got(block(rot_b, part, s, y, c), z_r.at[part, s])
+
+            @pl.when(z > 0)
+            def _():
+                down(part, s).start()
+
+            over_y(part, s).start()
+            over_core(part, s, 0).start()
+
+    def relay_y(part):
+        for s in others:
+            got(block(rot_b, part, s, 1 - y, c), y_r.at[part, s])
+            over_core(part, s, 1).start()
+
+    def rotate(part, s, first):
+        columns = pl.ds(pl.multiple_of(s * depth, depth), depth)
+        high, low = split(rot_b[part, s])
+        both = jnp.dot(orb_b[:, columns], high, preferred_element_type=F32)
+        cross = jnp.dot(orb_b[:elements * rows, columns], low, preferred_element_type=F32)
+        total = both[:elements * rows] + both[elements * rows:] + cross
+        acc_r[part] = total if first else acc_r[part] + total
+
+    def rotated(part):
+        for s in others:
+            for far in range(2):
+                got(block(rot_b, part, s, 1 - y if far else y, 1 - c), c_r.at[part, s, far])
+            rotate(part, s, False)
+        for i in range(elements):
+            place = lax.broadcasted_iota(jnp.int32, (rows, lanes), 0) + z * rows
+            alive = place < counts[i]
+            for b in range(n):
+                piece = acc_r[part, i * rows:(i + 1) * rows, b * lanes:(b + 1) * lanes]
+                res[part, b, i] = jnp.where(alive, piece, F32(0.0))
+        for to in others:
+            to_band(part, to).start()
+        start[part, :, pl.ds(pl.multiple_of(z * rows, rows), rows)] = res[part, z]
+        for copy in halo(0, part, z):
+            copy.start()
+
+    def spread(part):
+        for s in others:
+            got(rows_of(start, part, s), a_r.at[part, s])
+            for copy in halo(0, part, s):
+                copy.start()
+
+    def load(k, ref, part):
+        for i in range(elements):
+            high, low = split(ref[part, i])
+            field[k, i, :, :lanes] = high
+            field[k, i, :, lanes:] = low
+
+    def fold(r):
+        return (r[:basis, :lanes] + r[:basis, lanes:]) + (r[basis:, :lanes] + r[basis:, lanes:])
+
+    def local_slots(ref, part):
+        load(0, ref, part)
+
+        def body(i, carry):
+            r = jnp.dot(ham_b[i, 0], field[0, i], preferred_element_type=F32)
+            r += jnp.dot(ham_b[i, 1], field[0, lax.rem(i + elements - 1, elements)], preferred_element_type=F32)
+            r += jnp.dot(ham_b[i, 2], field[0, lax.rem(i + 1, elements)], preferred_element_type=F32)
+            acc[part, i] = fold(r)
+            return carry
+
+        lax.fori_loop(0, elements, body, 0)
+
+    def halo_slots(stage, part, done):
+        lo, hi = ((start_lo, start_hi), (mid_lo, mid_hi))[stage]
+        for s in range(n):
+            got(rows_of(lo, part, s), h_r.at[stage, part, s, 0])
+            got(rows_of(hi, part, s), h_r.at[stage, part, s, 1])
+        load(1, lo, part)
+        load(2, hi, part)
+
+        def body(i, carry):
+            r = jnp.dot(ham_b[i, 3], field[1, i], preferred_element_type=F32)
+            r += jnp.dot(ham_b[i, 4], field[2, i], preferred_element_type=F32)
+            done(i, acc[part, i] + fold(r))
+            return carry
+
+        lax.fori_loop(0, elements, body, 0)
+
+    send_own(0)
+    high, low = split(orb[...])
+    orb_b[:elements * rows] = high
+    orb_b[elements * rows:] = low
+    relay(0, 1)
+    send_own(1)
+    rotate(0, z, True)
+    relay(0, 2)
+    relay(0, 3)
+    relay(1, 1)
+    relay_y(0)
+    relay(1, 2)
+    rotated(0)
+    relay(1, 3)
+    relay_y(1)
+    rotate(1, z, True)
+    rotated(1)
+    spread(0)
+
+    ham_copy.wait()
+
+    def prepare(i, carry):
+        square = (basis, basis)
+        place = lax.broadcasted_iota(jnp.int32, square, 0)
+        scale = jnp.where(place < counts[i], 1.0 / jnp.full(square, width[0], F32), F32(0.0))
+        diagonal = jnp.where(place == lax.broadcasted_iota(jnp.int32, square, 1), center[0], F32(0.0))
+        for slot in range(SLOTS):
+            entries = ham_v[i, slot]
+            if slot == 0:
+                entries = entries - diagonal
+            high, low = split(entries * scale)
+            ham_b[i, slot, :basis] = high
+            ham_b[i, slot, basis:] = low
+        return carry
+
+    lax.fori_loop(0, elements, prepare, 0)
+    local_slots(start, 0)
+    spread(1)
+
+    def keep(part):
+        def done(i, total):
+            mid[part, i] = total
+        return done
+
+    def finish(part):
+        def done(i, total):
+            out[i, :, part * lanes:(part + 1) * lanes] = 2.0 * total - start[part, i]
+        return done
+
+    halo_slots(0, 0, keep(0))
+    for s in range(n):
+        for copy in halo(1, 0, s):
+            copy.start()
+    local_slots(start, 1)
+    halo_slots(0, 1, keep(1))
+    for s in range(n):
+        for copy in halo(1, 1, s):
+            copy.start()
+    local_slots(mid, 0)
+    halo_slots(1, 0, finish(0))
+    local_slots(mid, 1)
+    halo_slots(1, 1, finish(1))
+
+    for part in range(PARTS):
+        for s in range(n):
+            for stage in range(2):
+                for copy in halo(stage, part, s):
+                    copy.wait_send()
+
+            @pl.when((s <= z) & (z < n - 1))
+            def _():
+                up(part, s).wait_send()
+
+            @pl.when((s >= z) & (z > 0))
+            def _():
+                down(part, s).wait_send()
+
+        for s in others:
+            over_y(part, s).wait_send()
+            for far in range(2):
+                over_core(part, s, far).wait_send()
+            to_band(part, s).wait_send()
+
+
+def shards(orbitals, rotation, counts, hamiltonian, filter_center, filter_width):
+    elements, rows, bands = orbitals.shape
+    basis = hamiltonian.shape[2]
+    depth = rotation.shape[0]
+    n = bands // depth
+    lanes = depth // PARTS
+    own = (PARTS, elements, basis, lanes)
+    dma = pltpu.SemaphoreType.DMA
+    in_vmem = pl.BlockSpec(memory_space=pltpu.VMEM)
+    in_smem = pl.BlockSpec(memory_space=pltpu.SMEM)
+    flops = 2 * elements * rows * bands * bands * 3 + 2 * 2 * elements * SLOTS * basis * basis * depth * 4
+    return pl.pallas_call(
+        functools.partial(kernel, n),
+        out_shape=jax.ShapeDtypeStruct((elements, basis, depth), F32),
+        in_specs=[in_vmem, in_vmem, in_smem, in_smem, in_smem, pl.BlockSpec(memory_space=pl.ANY)],
+        out_specs=in_vmem,
+        scratch_shapes=[
+            pltpu.VMEM((elements, SLOTS, basis, basis), F32),
+            pltpu.VMEM((elements, SLOTS, 2 * basis, basis), BF16),
+            pltpu.VMEM((2 * elements * rows, bands), BF16),
+            pltpu.VMEM((PARTS, n, depth, n * lanes), F32),
+            pltpu.VMEM((PARTS, n, elements, rows, lanes), F32),
+            pltpu.VMEM((PARTS, elements * rows, n * lanes), F32),
+            pltpu.VMEM(own, F32), pltpu.VMEM(own, F32), pltpu.VMEM(own, F32),
+            pltpu.VMEM(own, F32), pltpu.VMEM(own, F32), pltpu.VMEM(own, F32),
+            pltpu.VMEM((3, elements, basis, 2 * lanes), BF16),
+            pltpu.VMEM(own, F32),
+            dma(()),
+            dma((PARTS, n)), dma((PARTS, n)), dma((PARTS, n)),
+            dma((PARTS, n)), dma((PARTS, n)),
+            dma((PARTS, n, 2)), dma((PARTS, n, 2)),
+            dma((PARTS, n)), dma((PARTS, n)),
+            dma((2, PARTS, n, 2)), dma((2, PARTS, n, 2)),
+        ],
+        compiler_params=pltpu.CompilerParams(
+            collective_id=0, has_side_effects=True, vmem_limit_bytes=48 * 1024 * 1024
+        ),
+        cost_estimate=pl.CostEstimate(flops=flops, bytes_accessed=8 * 1024 * 1024, transcendentals=0),
+    )(orbitals.reshape(elements * rows, bands), rotation, counts, filter_center, filter_width, hamiltonian)
+
+
 def solution(mesh):
+    fits = mesh.shape["elem"] == GY and mesh.shape["band"] == 4
     return jax.shard_map(
-        shards,
+        shards if fits else general_shards,
         mesh=mesh,
         in_specs=(
             P("elem", "band", None),

time: 177 us -> 72 us (0.41)
  waiting for transfers between devices: 128 us -> 0 us
  Pallas kernels: 0 us -> 66.7 us
  between operations: 14.9 us -> 1.32 us
  matrix products: 11.4 us -> 0 us
  local copies, waits for them, and re-layouts: 11.1 us -> 3.8 us
  starting transfers between devices: 6.25 us -> 0 us
  other arithmetic: 4.91 us -> 0 us
    all_gather x1 -> x0, waiting for transfers between devices: 85.2 us -> none  [shards(): whole_rotation = lax.all_gather(rotation, 'band', axis=0, tiled=True)]
    pallas_call x0 -> x1, Pallas kernels: none -> 66.7 us  [shards(): pl.pallas_call(functools.partial(kernel, n), out_shape=jax.ShapeDtypeStru...]
    ppermute x4 -> x0, waiting for transfers between devices: 25.8 us -> none  [the longest x2 24.2 us: neighbour_rows(): lax.ppermute(field, 'elem', ahead)]
    all_to_all x1 -> x0, waiting for transfers between devices: 16.2 us -> none  [shards(): lax.all_to_all(rotated, 'band', split_axis=2, concat_axis=1, tiled=True)]
    dot_general x11 -> x0, matrix products: 11.4 us -> none  [the longest x10 7.76 us: apply_operator(): jnp.einsum('erc,ecb->erb', hamiltonian[:, slot], other, precision=lax.Pre...]
    unnamed x10 -> x7, local copies, waits for them, and re-layouts: 7.97 us -> 3.8 us
    all_to_all x1 -> x0, starting transfers between devices: 3.48 us -> none  [shards(): lax.all_to_all(rotated, 'band', split_axis=2, concat_axis=1, tiled=True)]
    all_to_all x1 -> x0, other arithmetic: 3.45 us -> none  [shards(): lax.all_to_all(rotated, 'band', split_axis=2, concat_axis=1, tiled=True)]
  transfers between devices with their start and end apart: 6 -> 0, of which waited for: 6 -> 0; matrix products, arithmetic and copies ran while one was open for 3% -> 0% of each run, Pallas kernels for 0% -> 0%
where the time goes in v2:
time: 72 us; the launch traced here: 71.8 us
  Pallas kernels  66.7 us (93%)
  local copies, waits for them, and re-layouts  3.8 us (5%)
  between operations  1.32 us (2%)
    pallas_call x1, Pallas kernels, shards(): pl.pallas_call(functools.partial(kernel, n), out_shape=jax.ShapeDtypeStru...  66.7 us
    unnamed x7, local copies, waits for them, and re-layouts  3.8 us

profile of v2, /device:TPU:0, one launch (start us, length us, event | category | flops | bytes accessed | tf_op | source)
XLA Modules:
  0.0 71.8 jit_solution(12799881635471275731)
XLA Ops:
  1.3 0.0 copy-start
  1.3 1.2 %copy-done = f32[256,1024]{1,0:T(8,128)S(1)} copy-done((f32[256,1024]{1,0:T(8,128)S(1)}, f32[256,1024]{1,0:T(8,128)}, u32[]{:S(2)}) %copy-start) | copy-done | bytes 1048600
  2.5 0.0 copy-start.1
  2.5 1.1 %copy-done.1 = f32[4,40,1024]{2,1,0:T(8,128)S(1)} copy-done((f32[4,40,1024]{2,1,0:T(8,128)S(1)}, f32[4,40,1024]{2,1,0:T(8,128)}, u32[]{:S(2)}) %copy-start.1) | copy-done | bytes 655384
  3.6 0.0 copy-start.2
  3.6 0.7 copy-done.2
  4.3 66.7 %shard_map.64 = f32[4,160,256]{2,1,0:T(8,128)S(1)} custom-call(f32[160,1024]{1,0:T(8,128)S(1)} %bitcast.1, f32[256,1024]{1,0:T(8,128)S(1)} %copy-done, s32[4]{0:T(128)S(1)} %copy-done.2, f32[1]{0:T(128)S(6)} %copy.8.center, f32[1]{0:T(128)S(6)} %copy.9.width, f32[4,7,160,160]{3,2,1,0:T(8,128)} %ham.1), custom_call_target="tpu_custom_call" | custom-call | flops 3103784960 | bytes 8388608 | tf_op jit(solution)/shard_map/pallas_call | solution.py:344
  71.0 0.8 %copy.10 = f32[4,160,256]{2,1,0:T(8,128)} copy(f32[4,160,256]{2,1,0:T(8,128)S(1)} %shard_map.64) | data formatting | bytes 1310720
Async XLA Ops:
  1.3 1.2 %copy-start = (f32[256,1024]{1,0:T(8,128)S(1)}, f32[256,1024]{1,0:T(8,128)}, u32[]{:S(2)}) copy-start(f32[256,1024]{1,0:T(8,128)} %rot.1) | copy-start | bytes 3145732
  2.5 1.1 %copy-start.1 = (f32[4,40,1024]{2,1,0:T(8,128)S(1)}, f32[4,40,1024]{2,1,0:T(8,128)}, u32[]{:S(2)}) copy-start(f32[4,40,1024]{2,1,0:T(8,128)} %param.6) | copy-start | bytes 1966084
  3.6 0.7 copy-start.2

commit v3 on v2

--- a/solution.py
+++ b/solution.py
@@ -65,8 +65,8 @@
 
 def kernel(
     n, orb, rot, counts, center, width, ham, out,
-    ham_v, ham_b, orb_b, rot_b, res, acc_r, start, start_lo, start_hi, mid, mid_lo, mid_hi,
-    field, acc, ham_sem,
+    ham_v, ham_b, orb_v, orb_b, rot_b, res, acc_r, start, start_lo, start_hi, mid, mid_lo, mid_hi,
+    field, acc, ham_sem, orb_sem, rot_sem,
     up_s, dn_s, z_r, y_s, y_r, c_s, c_r, a_s, a_r, h_s, h_r,
 ):
     e, z = lax.axis_index("elem"), lax.axis_index("band")
@@ -110,22 +110,20 @@
     def got(dst, recv):
         remote(dst, dst, recv, recv, twin, z).wait_recv()
 
-    def to_band(part, to):
+    def rows_of(part, i, s):
+        return start.at[part, i, pl.ds(pl.multiple_of(s * rows, rows), rows)]
+
+    def to_band(part, i, to):
         return remote(
-            res.at[part, to],
-            start.at[part, :, pl.ds(pl.multiple_of(z * rows, rows), rows)],
-            a_s.at[part, to], a_r.at[part, z], e, to,
-        )
-
-    def rows_of(ref, part, s):
-        return ref.at[part, :, pl.ds(pl.multiple_of(s * rows, rows), rows)]
-
-    def halo(stage, part, s):
+            res.at[part, to, i], rows_of(part, i, z), a_s.at[part, i, to], a_r.at[part, i, z], e, to
+        )
+
+    def halo(stage, part, i):
         own, lo, hi = ((start, start_lo, start_hi), (mid, mid_lo, mid_hi))[stage]
-        b = rows_of(own, part, s)
+        b = own.at[part, i]
         return (
-            remote(b, rows_of(lo, part, s), h_s.at[stage, part, s, 0], h_r.at[stage, part, s, 0], ahead, z),
-            remote(b, rows_of(hi, part, s), h_s.at[stage, part, s, 1], h_r.at[stage, part, s, 1], behind, z),
+            remote(b, lo.at[part, i], h_s.at[stage, part, i, 0], h_r.at[stage, part, i, 0], ahead, z),
+            remote(b, hi.at[part, i], h_s.at[stage, part, i, 1], h_r.at[stage, part, i, 1], behind, z),
         )
 
     barrier = pltpu.get_barrier_semaphore()
@@ -133,13 +131,24 @@
     for elem, band in partners:
         pl.semaphore_signal(barrier, inc=1, device_id=(elem, band), device_id_type=pl.DeviceIdType.MESH)
     ham_copy = pltpu.make_async_copy(ham.at[:, pl.ds(0, SLOTS)], ham_v, ham_sem)
-    ham_copy.start()
-    for part in range(PARTS):
-        for b in range(n):
-            rot_b[part, z, :, b * lanes:(b + 1) * lanes] = rot[:, (b * PARTS + part) * lanes:(b * PARTS + part + 1) * lanes]
+    orb_copy = pltpu.make_async_copy(orb, orb_v, orb_sem)
+    rot_copies = [
+        pltpu.make_async_copy(
+            rot.at[:, pl.ds((b * PARTS + part) * lanes, lanes)],
+            rot_b.at[part, z, :, pl.ds(b * lanes, lanes)],
+            rot_sem.at[part, b],
+        )
+        for part in range(PARTS)
+        for b in range(n)
+    ]
+    for copy in rot_copies[:n] + [orb_copy] + rot_copies[n:] + [ham_copy]:
+        copy.start()
     pl.semaphore_wait(barrier, len(partners))
 
     def send_own(part):
+        for copy in rot_copies[part * n:(part + 1) * n]:
+            copy.wait()
+
         @pl.when(z < n - 1)
         def _():
             up(part, z).start()
@@ -197,29 +206,27 @@
             for b in range(n):
                 piece = acc_r[part, i * rows:(i + 1) * rows, b * lanes:(b + 1) * lanes]
                 res[part, b, i] = jnp.where(alive, piece, F32(0.0))
-        for to in others:
-            to_band(part, to).start()
-        start[part, :, pl.ds(pl.multiple_of(z * rows, rows), rows)] = res[part, z]
-        for copy in halo(0, part, z):
+            for to in others:
+                to_band(part, i, to).start()
+            start[part, i, pl.ds(pl.multiple_of(z * rows, rows), rows)] = res[part, z, i]
+
+    def spread(part, i):
+        for s in others:
+            got(rows_of(part, i, s), a_r.at[part, i, s])
+        for copy in halo(0, part, i):
             copy.start()
 
-    def spread(part):
-        for s in others:
-            got(rows_of(start, part, s), a_r.at[part, s])
-            for copy in halo(0, part, s):
-                copy.start()
-
-    def load(k, ref, part):
-        for i in range(elements):
-            high, low = split(ref[part, i])
-            field[k, i, :, :lanes] = high
-            field[k, i, :, lanes:] = low
+    def load(k, ref, part, i):
+        high, low = split(ref[part, i])
+        field[k, i, :, :lanes] = high
+        field[k, i, :, lanes:] = low
 
     def fold(r):
         return (r[:basis, :lanes] + r[:basis, lanes:]) + (r[basis:, :lanes] + r[basis:, lanes:])
 
     def local_slots(ref, part):
-        load(0, ref, part)
+        for i in range(elements):
+            load(0, ref, part, i)
 
         def body(i, carry):
             r = jnp.dot(ham_b[i, 0], field[0, i], preferred_element_type=F32)
@@ -230,91 +237,88 @@
 
         lax.fori_loop(0, elements, body, 0)
 
-    def halo_slots(stage, part, done):
+    def halo_slots(stage, part, i):
         lo, hi = ((start_lo, start_hi), (mid_lo, mid_hi))[stage]
-        for s in range(n):
-            got(rows_of(lo, part, s), h_r.at[stage, part, s, 0])
-            got(rows_of(hi, part, s), h_r.at[stage, part, s, 1])
-        load(1, lo, part)
-        load(2, hi, part)
-
-        def body(i, carry):
-            r = jnp.dot(ham_b[i, 3], field[1, i], preferred_element_type=F32)
-            r += jnp.dot(ham_b[i, 4], field[2, i], preferred_element_type=F32)
-            done(i, acc[part, i] + fold(r))
+        got(lo.at[part, i], h_r.at[stage, part, i, 0])
+        got(hi.at[part, i], h_r.at[stage, part, i, 1])
+        load(1, lo, part, i)
+        load(2, hi, part, i)
+        r = jnp.dot(ham_b[i, 3], field[1, i], preferred_element_type=F32)
+        r += jnp.dot(ham_b[i, 4], field[2, i], preferred_element_type=F32)
+        return acc[part, i] + fold(r)
+
+    def middle(part, i):
+        mid[part, i] = halo_slots(0, part, i)
+        for copy in halo(1, part, i):
+            copy.start()
+
+    def finish(part, i):
+        out[i, :, part * lanes:(part + 1) * lanes] = 2.0 * halo_slots(1, part, i) - start[part, i]
+
+    def prepare_all():
+        ham_copy.wait()
+
+        def prepare(i, carry):
+            square = (basis, basis)
+            place = lax.broadcasted_iota(jnp.int32, square, 0)
+            scale = jnp.where(place < counts[i], 1.0 / jnp.full(square, width[0], F32), F32(0.0))
+            diagonal = jnp.where(place == lax.broadcasted_iota(jnp.int32, square, 1), center[0], F32(0.0))
+            for slot in range(SLOTS):
+                entries = ham_v[i, slot]
+                if slot == 0:
+                    entries = entries - diagonal
+                high, low = split(entries * scale)
+                ham_b[i, slot, :basis] = high
+                ham_b[i, slot, basis:] = low
             return carry
 
-        lax.fori_loop(0, elements, body, 0)
+        lax.fori_loop(0, elements, prepare, 0)
 
     send_own(0)
-    high, low = split(orb[...])
+    orb_copy.wait()
+    high, low = split(orb_v[...])
     orb_b[:elements * rows] = high
     orb_b[elements * rows:] = low
+    rotate(0, z, True)
     relay(0, 1)
+    relay(0, 2)
     send_own(1)
-    rotate(0, z, True)
-    relay(0, 2)
     relay(0, 3)
+    prepare_all()
+    relay_y(0)
+    rotated(0)
     relay(1, 1)
-    relay_y(0)
     relay(1, 2)
-    rotated(0)
     relay(1, 3)
+    rotate(1, z, True)
     relay_y(1)
-    rotate(1, z, True)
+    spread(0, 0)
+    spread(0, 1)
     rotated(1)
-    spread(0)
-
-    ham_copy.wait()
-
-    def prepare(i, carry):
-        square = (basis, basis)
-        place = lax.broadcasted_iota(jnp.int32, square, 0)
-        scale = jnp.where(place < counts[i], 1.0 / jnp.full(square, width[0], F32), F32(0.0))
-        diagonal = jnp.where(place == lax.broadcasted_iota(jnp.int32, square, 1), center[0], F32(0.0))
-        for slot in range(SLOTS):
-            entries = ham_v[i, slot]
-            if slot == 0:
-                entries = entries - diagonal
-            high, low = split(entries * scale)
-            ham_b[i, slot, :basis] = high
-            ham_b[i, slot, basis:] = low
-        return carry
-
-    lax.fori_loop(0, elements, prepare, 0)
+    for i in range(2, elements):
+        spread(0, i)
     local_slots(start, 0)
-    spread(1)
-
-    def keep(part):
-        def done(i, total):
-            mid[part, i] = total
-        return done
-
-    def finish(part):
-        def done(i, total):
-            out[i, :, part * lanes:(part + 1) * lanes] = 2.0 * total - start[part, i]
-        return done
-
-    halo_slots(0, 0, keep(0))
-    for s in range(n):
-        for copy in halo(1, 0, s):
-            copy.start()
+    for i in range(elements):
+        middle(0, i)
+        spread(1, i)
     local_slots(start, 1)
-    halo_slots(0, 1, keep(1))
-    for s in range(n):
-        for copy in halo(1, 1, s):
-            copy.start()
+    for i in range(elements):
+        middle(1, i)
     local_slots(mid, 0)
-    halo_slots(1, 0, finish(0))
+    for i in range(elements):
+        finish(0, i)
     local_slots(mid, 1)
-    halo_slots(1, 1, finish(1))
+    for i in range(elements):
+        finish(1, i)
 
     for part in range(PARTS):
+        for i in range(elements):
+            for stage in range(2):
+                for copy in halo(stage, part, i):
+                    copy.wait_send()
+            for to in others:
+                to_band(part, i, to).wait_send()
         for s in range(n):
-            for stage in range(2):
-                for copy in halo(stage, part, s):
-                    copy.wait_send()
-
             @pl.when((s <= z) & (z < n - 1))
             def _():
                 up(part, s).wait_send()
@@ -327,7 +331,6 @@
             over_y(part, s).wait_send()
             for far in range(2):
                 over_core(part, s, far).wait_send()
-            to_band(part, s).wait_send()
 
 
 def shards(orbitals, rotation, counts, hamiltonian, filter_center, filter_width):
@@ -339,16 +342,18 @@
     own = (PARTS, elements, basis, lanes)
     dma = pltpu.SemaphoreType.DMA
     in_vmem = pl.BlockSpec(memory_space=pltpu.VMEM)
+    in_hbm = pl.BlockSpec(memory_space=pltpu.HBM)
     in_smem = pl.BlockSpec(memory_space=pltpu.SMEM)
     flops = 2 * elements * rows * bands * bands * 3 + 2 * 2 * elements * SLOTS * basis * basis * depth * 4
     return pl.pallas_call(
         functools.partial(kernel, n),
         out_shape=jax.ShapeDtypeStruct((elements, basis, depth), F32),
-        in_specs=[in_vmem, in_vmem, in_smem, in_smem, in_smem, pl.BlockSpec(memory_space=pl.ANY)],
+        in_specs=[in_hbm, in_hbm, in_smem, in_smem, in_smem, in_hbm],
         out_specs=in_vmem,
         scratch_shapes=[
             pltpu.VMEM((elements, SLOTS, basis, basis), F32),
             pltpu.VMEM((elements, SLOTS, 2 * basis, basis), BF16),
+            pltpu.VMEM((elements * rows, bands), F32),
             pltpu.VMEM((2 * elements * rows, bands), BF16),
             pltpu.VMEM((PARTS, n, depth, n * lanes), F32),
             pltpu.VMEM((PARTS, n, elements, rows, lanes), F32),
@@ -357,15 +362,15 @@
             pltpu.VMEM(own, F32), pltpu.VMEM(own, F32), pltpu.VMEM(own, F32),
             pltpu.VMEM((3, elements, basis, 2 * lanes), BF16),
             pltpu.VMEM(own, F32),
-            dma(()),
+            dma(()), dma(()), dma((PARTS, n)),
             dma((PARTS, n)), dma((PARTS, n)), dma((PARTS, n)),
             dma((PARTS, n)), dma((PARTS, n)),
             dma((PARTS, n, 2)), dma((PARTS, n, 2)),
-            dma((PARTS, n)), dma((PARTS, n)),
-            dma((2, PARTS, n, 2)), dma((2, PARTS, n, 2)),
+            dma((PARTS, elements, n)), dma((PARTS, elements, n)),
+            dma((2, PARTS, elements, 2)), dma((2, PARTS, elements, 2)),
         ],
         compiler_params=pltpu.CompilerParams(
-            collective_id=0, has_side_effects=True, vmem_limit_bytes=48 * 1024 * 1024
+            collective_id=0, has_side_effects=True, vmem_limit_bytes=63 * 1024 * 1024
         ),
         cost_estimate=pl.CostEstimate(flops=flops, bytes_accessed=8 * 1024 * 1024, transcendentals=0),
     )(orbitals.reshape(elements * rows, bands), rotation, counts, filter_center, filter_width, hamiltonian)

time: 72 us -> 77 us (1.069)
  Pallas kernels: 66.7 us -> 73.6 us
  local copies, waits for them, and re-layouts: 3.8 us -> 1.98 us
    pallas_call x1, Pallas kernels: 66.7 us -> 73.6 us  [shards(): pl.pallas_call(functools.partial(kernel, n), out_shape=jax.ShapeDtypeStru...]
    unnamed x7 -> x1, local copies, waits for them, and re-layouts: 3.8 us -> 1.98 us
where the time goes in v3:
time: 77 us; the launch traced here: 76.8 us
  Pallas kernels  73.6 us (96%)
  local copies, waits for them, and re-layouts  1.98 us (3%)
  between operations  1.3 us (2%)
    pallas_call x1, Pallas kernels, shards(): pl.pallas_call(functools.partial(kernel, n), out_shape=jax.ShapeDtypeStru...  73.6 us
    unnamed x1, local copies, waits for them, and re-layouts  1.98 us

profile of v3, /device:TPU:0, one launch (start us, length us, event | category | flops | bytes accessed | tf_op | source)
XLA Modules:
  0.0 76.8 jit_solution(18243028750731683316)
XLA Ops:
  1.3 73.6 %shard_map.64 = f32[4,160,256]{2,1,0:T(8,128)} custom-call(f32[160,1024]{1,0:T(8,128)} %bitcast.1, f32[256,1024]{1,0:T(8,128)} %rot.1, s32[4]{0:T(128)} %counts.1, f32[1]{0:T(128)S(6)} %copy.8.center, f32[1]{0:T(128)S(6)} %copy.9.width, f32[4,7,160,160]{3,2,1,0:T(8,128)} %ham.1), custom_call_target="tpu_custom_call" | custom-call | flops 3103784960 | bytes 8388608 | tf_op jit(solution)/shard_map/pallas_call | solution.py:348
  74.9 2.0 %copy.10 = f32[4,160,256]{2,1,0:T(8,128)} copy(f32[4,160,256]{2,1,0:T(8,128)} %shard_map.64) | data formatting | bytes 1310720

commit v4 on v3

--- a/solution.py
+++ b/solution.py
@@ -67,17 +67,19 @@
     n, orb, rot, counts, center, width, ham, out,
     ham_v, ham_b, orb_v, orb_b, rot_b, res, acc_r, start, start_lo, start_hi, mid, mid_lo, mid_hi,
     field, acc, ham_sem, orb_sem, rot_sem,
-    up_s, dn_s, z_r, y_s, y_r, c_s, c_r, a_s, a_r, h_s, h_r,
+    g_s, g_r, c_s, c_r, a_s, a_r, b_s, b_r, h_s, h_r,
 ):
     e, z = lax.axis_index("elem"), lax.axis_index("band")
     elements, basis = ham.shape[0], ham.shape[2]
     rows = basis // n
     depth = rot.shape[0]
     lanes = start.shape[3]
-    share = depth // 4
-    y, c = e // 4, e % 2
+    share = depth // 8
+    x, c = (e // 2) % 2, e % 2
     ahead, behind = lax.rem(e + 1, 8), lax.rem(e + 7, 8)
-    across, twin = lax.rem(e + 4, 8), e + 1 - 2 * c
+    beside, across, twin = e + 2 - 4 * x, lax.rem(e + 4, 8), e + 1 - 2 * c
+    diagonal = lax.rem(beside + 4, 8)
+    planes = (e, beside, across, diagonal)
     others = [lax.rem(z + j, n) for j in range(1, n)]
 
     def remote(src, dst, send, recv, elem, band):
@@ -86,48 +88,58 @@
             device_id=(elem, band), device_id_type=pl.DeviceIdType.MESH,
         )
 
-    def block(ref, part, s, yy, cc):
-        first = pl.multiple_of((yy * 2 + cc) * share, share)
-        return ref.at[part, s, pl.ds(first, share)]
-
-    def up(part, s):
-        b = block(rot_b, part, s, y, c)
-        return remote(b, b, up_s.at[part, s], z_r.at[part, s], e, z + 1)
-
-    def down(part, s):
-        b = block(rot_b, part, s, y, c)
-        return remote(b, b, dn_s.at[part, s], z_r.at[part, s], e, z - 1)
+    def eighth(part, s, owner):
+        return rot_b.at[part, s, pl.ds(pl.multiple_of(owner * share, share), share)]
+
+    def over_z(part, to):
+        b = eighth(part, z, e)
+        return remote(b, b, g_s.at[0, part, to], g_r.at[0, part, z], e, to)
+
+    def over_x(part, s):
+        b = eighth(part, s, e)
+        return remote(b, b, g_s.at[1, part, s], g_r.at[1, part, s], beside, z)
 
     def over_y(part, s):
-        b = block(rot_b, part, s, y, c)
-        return remote(b, b, y_s.at[part, s], y_r.at[part, s], across, z)
-
-    def over_core(part, s, far):
-        yy = 1 - y if far else y
-        b = block(rot_b, part, s, yy, c)
-        return remote(b, b, c_s.at[part, s, far], c_r.at[part, s, far], twin, z)
+        b = eighth(part, s, e)
+        return remote(b, b, g_s.at[2, part, s], g_r.at[2, part, s], across, z)
+
+    def relay_over_y(part, s):
+        b = eighth(part, s, beside)
+        return remote(b, b, g_s.at[3, part, s], g_r.at[3, part, s], across, z)
+
+    def relay_over_x(part, s):
+        b = eighth(part, s, across)
+        return remote(b, b, g_s.at[3, part, s], g_r.at[3, part, s], beside, z)
+
+    def over_core(part, s, k):
+        b = eighth(part, s, planes[k])
+        return remote(b, b, c_s.at[part, s, k], c_r.at[part, s, k], twin, z)
 
     def got(dst, recv):
         remote(dst, dst, recv, recv, twin, z).wait_recv()
 
-    def rows_of(part, i, s):
-        return start.at[part, i, pl.ds(pl.multiple_of(s * rows, rows), rows)]
-
-    def to_band(part, i, to):
-        return remote(
-            res.at[part, to, i], rows_of(part, i, z), a_s.at[part, i, to], a_r.at[part, i, z], e, to
-        )
-
-    def halo(stage, part, i):
-        own, lo, hi = ((start, start_lo, start_hi), (mid, mid_lo, mid_hi))[stage]
-        b = own.at[part, i]
+    def rows_of(ref, part, s):
+        return ref.at[part, :, pl.ds(pl.multiple_of(s * rows, rows), rows)]
+
+    def to_band(part, to):
+        return remote(res.at[part, to], rows_of(start, part, z), a_s.at[part, to], a_r.at[part, z], e, to)
+
+    def start_halo(part, s):
+        b = rows_of(start, part, s)
         return (
-            remote(b, lo.at[part, i], h_s.at[stage, part, i, 0], h_r.at[stage, part, i, 0], ahead, z),
-            remote(b, hi.at[part, i], h_s.at[stage, part, i, 1], h_r.at[stage, part, i, 1], behind, z),
+            remote(b, rows_of(start_lo, part, s), b_s.at[part, s, 0], b_r.at[part, s, 0], ahead, z),
+            remote(b, rows_of(start_hi, part, s), b_s.at[part, s, 1], b_r.at[part, s, 1], behind, z),
+        )
+
+    def mid_halo(part, i):
+        b = mid.at[part, i]
+        return (
+            remote(b, mid_lo.at[part, i], h_s.at[part, i, 0], h_r.at[part, i, 0], ahead, z),
+            remote(b, mid_hi.at[part, i], h_s.at[part, i, 1], h_r.at[part, i, 1], behind, z),
         )
 
     barrier = pltpu.get_barrier_semaphore()
-    partners = [(ahead, z), (behind, z), (across, z)] + [(e, other) for other in others]
+    partners = [(ahead, z), (behind, z), (beside, z), (across, z)] + [(e, other) for other in others]
     for elem, band in partners:
         pl.semaphore_signal(barrier, inc=1, device_id=(elem, band), device_id_type=pl.DeviceIdType.MESH)
     ham_copy = pltpu.make_async_copy(ham.at[:, pl.ds(0, SLOTS)], ham_v, ham_sem)
@@ -148,44 +160,36 @@
     def send_own(part):
         for copy in rot_copies[part * n:(part + 1) * n]:
             copy.wait()
-
-        @pl.when(z < n - 1)
-        def _():
-            up(part, z).start()
-
-        @pl.when(z > 0)
-        def _():
-            down(part, z).start()
-
-    def relay(part, d):
-        @pl.when(z >= d)
-        def _():
-            s = z - d
-            got(block(rot_b, part, s, y, c), z_r.at[part, s])
-
-            @pl.when(z < n - 1)
-            def _():
-                up(part, s).start()
-
+        for to in others:
+            over_z(part, to).start()
+
+    def gather_first(part):
+        for s in others:
+            got(eighth(part, s, e), g_r.at[0, part, s])
+            over_x(part, s).start()
             over_y(part, s).start()
             over_core(part, s, 0).start()
 
-        @pl.when(z + d < n)
-        def _():
-            s = z + d
-            got(block(rot_b, part, s, y, c), z_r.at[part, s])
-
-            @pl.when(z > 0)
+    def gather_second(part):
+        for s in others:
+            got(eighth(part, s, beside), g_r.at[1, part, s])
+            got(eighth(part, s, across), g_r.at[2, part, s])
+
+            @pl.when(c == 0)
             def _():
-                down(part, s).start()
-
-            over_y(part, s).start()
-            over_core(part, s, 0).start()
-
-    def relay_y(part):
-        for s in others:
-            got(block(rot_b, part, s, 1 - y, c), y_r.at[part, s])
+                relay_over_y(part, s).start()
+
+            @pl.when(c == 1)
+            def _():
+                relay_over_x(part, s).start()
+
             over_core(part, s, 1).start()
+            over_core(part, s, 2).start()
+
+    def gather_third(part):
+        for s in others:
+            got(eighth(part, s, diagonal), g_r.at[3, part, s])
+            over_core(part, s, 3).start()
 
     def rotate(part, s, first):
         columns = pl.ds(pl.multiple_of(s * depth, depth), depth)
@@ -197,8 +201,8 @@
 
     def rotated(part):
         for s in others:
-            for far in range(2):
-                got(block(rot_b, part, s, 1 - y if far else y, 1 - c), c_r.at[part, s, far])
+            for k in range(4):
+                got(eighth(part, s, planes[k] + 1 - 2 * c), c_r.at[part, s, k])
             rotate(part, s, False)
         for i in range(elements):
             place = lax.broadcasted_iota(jnp.int32, (rows, lanes), 0) + z * rows
@@ -206,15 +210,17 @@
             for b in range(n):
                 piece = acc_r[part, i * rows:(i + 1) * rows, b * lanes:(b + 1) * lanes]
                 res[part, b, i] = jnp.where(alive, piece, F32(0.0))
-            for to in others:
-                to_band(part, i, to).start()
-            start[part, i, pl.ds(pl.multiple_of(z * rows, rows), rows)] = res[part, z, i]
-
-    def spread(part, i):
-        for s in others:
-            got(rows_of(part, i, s), a_r.at[part, i, s])
-        for copy in halo(0, part, i):
+        for to in others:
+            to_band(part, to).start()
+        start[part, :, pl.ds(pl.multiple_of(z * rows, rows), rows)] = res[part, z]
+        for copy in start_halo(part, z):
             copy.start()
+
+    def spread(part):
+        for s in others:
+            got(rows_of(start, part, s), a_r.at[part, s])
+            for copy in start_halo(part, s):
+                copy.start()
 
     def load(k, ref, part, i):
         high, low = split(ref[part, i])
@@ -237,23 +243,28 @@
 
         lax.fori_loop(0, elements, body, 0)
 
-    def halo_slots(stage, part, i):
-        lo, hi = ((start_lo, start_hi), (mid_lo, mid_hi))[stage]
-        got(lo.at[part, i], h_r.at[stage, part, i, 0])
-        got(hi.at[part, i], h_r.at[stage, part, i, 1])
+    def halo_slots(lo, hi, part, i):
         load(1, lo, part, i)
         load(2, hi, part, i)
         r = jnp.dot(ham_b[i, 3], field[1, i], preferred_element_type=F32)
         r += jnp.dot(ham_b[i, 4], field[2, i], preferred_element_type=F32)
         return acc[part, i] + fold(r)
 
-    def middle(part, i):
-        mid[part, i] = halo_slots(0, part, i)
-        for copy in halo(1, part, i):
-            copy.start()
-
-    def finish(part, i):
-        out[i, :, part * lanes:(part + 1) * lanes] = 2.0 * halo_slots(1, part, i) - start[part, i]
+    def middle(part):
+        for s in range(n):
+            got(rows_of(start_lo, part, s), b_r.at[part, s, 0])
+            got(rows_of(start_hi, part, s), b_r.at[part, s, 1])
+        for i in range(elements):
+            mid[part, i] = halo_slots(start_lo, start_hi, part, i)
+            for copy in mid_halo(part, i):
+                copy.start()
+
+    def finish(part):
+        for i in range(elements):
+            got(mid_lo.at[part, i], h_r.at[part, i, 0])
+            got(mid_hi.at[part, i], h_r.at[part, i, 1])
+            total = halo_slots(mid_lo, mid_hi, part, i)
+            out[i, :, part * lanes:(part + 1) * lanes] = 2.0 * total - start[part, i]
 
     def prepare_all():
         ham_copy.wait()
@@ -275,62 +286,48 @@
         lax.fori_loop(0, elements, prepare, 0)
 
     send_own(0)
+    send_own(1)
     orb_copy.wait()
     high, low = split(orb_v[...])
     orb_b[:elements * rows] = high
     orb_b[elements * rows:] = low
     rotate(0, z, True)
-    relay(0, 1)
-    relay(0, 2)
-    send_own(1)
-    relay(0, 3)
+    gather_first(0)
+    gather_second(0)
+    gather_first(1)
+    gather_third(0)
+    gather_second(1)
+    rotated(0)
+    gather_third(1)
+    rotate(1, z, True)
+    rotated(1)
+    spread(0)
     prepare_all()
-    relay_y(0)
-    rotated(0)
-    relay(1, 1)
-    relay(1, 2)
-    relay(1, 3)
-    rotate(1, z, True)
-    relay_y(1)
-    spread(0, 0)
-    spread(0, 1)
-    rotated(1)
-    for i in range(2, elements):
-        spread(0, i)
     local_slots(start, 0)
-    for i in range(elements):
-        middle(0, i)
-        spread(1, i)
+    spread(1)
+    middle(0)
     local_slots(start, 1)
-    for i in range(elements):
-        middle(1, i)
+    middle(1)
     local_slots(mid, 0)
-    for i in range(elements):
-        finish(0, i)
+    finish(0)
     local_slots(mid, 1)
-    for i in range(elements):
-        finish(1, i)
+    finish(1)
 
     for part in range(PARTS):
         for i in range(elements):
-            for stage in range(2):
-                for copy in halo(stage, part, i):
-                    copy.wait_send()
-            for to in others:
-                to_band(part, i, to).wait_send()
+            for copy in mid_halo(part, i):
+                copy.wait_send()
         for s in range(n):
-            @pl.when((s <= z) & (z < n - 1))
-            def _():
-                up(part, s).wait_send()
-
-            @pl.when((s >= z) & (z > 0))
-            def _():
-                down(part, s).wait_send()
-
-        for s in others:
+            for copy in start_halo(part, s):
+                copy.wait_send()
+        for s in others:
+            over_z(part, s).wait_send()
+            over_x(part, s).wait_send()
             over_y(part, s).wait_send()
-            for far in range(2):
-                over_core(part, s, far).wait_send()
+            relay_over_y(part, s).wait_send()
+            for k in range(4):
+                over_core(part, s, k).wait_send()
+            to_band(part, s).wait_send()
 
 
 def shards(orbitals, rotation, counts, hamiltonian, filter_center, filter_width):
@@ -363,11 +360,11 @@
             pltpu.VMEM((3, elements, basis, 2 * lanes), BF16),
             pltpu.VMEM(own, F32),
             dma(()), dma(()), dma((PARTS, n)),
-            dma((PARTS, n)), dma((PARTS, n)), dma((PARTS, n)),
+            dma((4, PARTS, n)), dma((4, PARTS, n)),
+            dma((PARTS, n, 4)), dma((PARTS, n, 4)),
             dma((PARTS, n)), dma((PARTS, n)),
             dma((PARTS, n, 2)), dma((PARTS, n, 2)),
-            dma((PARTS, elements, n)), dma((PARTS, elements, n)),
-            dma((2, PARTS, elements, 2)), dma((2, PARTS, elements, 2)),
+            dma((PARTS, elements, 2)), dma((PARTS, elements, 2)),
         ],
         compiler_params=pltpu.CompilerParams(
             collective_id=0, has_side_effects=True, vmem_limit_bytes=63 * 1024 * 1024

time: 77 us -> 67.3 us (0.87)
  Pallas kernels: 73.6 us -> 63.1 us
    pallas_call x1, Pallas kernels: 73.6 us -> 63.1 us  [shards(): pl.pallas_call(functools.partial(kernel, n), out_shape=jax.ShapeDtypeStru...]
where the time goes in v4:
time: 67.3 us; the launch traced here: 66.4 us
  Pallas kernels  63.1 us (94%)
  local copies, waits for them, and re-layouts  1.98 us (3%)
  between operations  1.3 us (2%)
    pallas_call x1, Pallas kernels, shards(): pl.pallas_call(functools.partial(kernel, n), out_shape=jax.ShapeDtypeStru...  63.1 us
    unnamed x1, local copies, waits for them, and re-layouts  1.98 us

profile of v4, /device:TPU:0, one launch (start us, length us, event | category | flops | bytes accessed | tf_op | source)
XLA Modules:
  0.0 66.4 jit_solution(17795487232396703739)
XLA Ops:
  1.3 63.1 %shard_map.64 = f32[4,160,256]{2,1,0:T(8,128)} custom-call(f32[160,1024]{1,0:T(8,128)} %bitcast.1, f32[256,1024]{1,0:T(8,128)} %rot.1, s32[4]{0:T(128)} %counts.1, f32[1]{0:T(128)S(6)} %copy.8.center, f32[1]{0:T(128)S(6)} %copy.9.width, f32[4,7,160,160]{3,2,1,0:T(8,128)} %ham.1), custom_call_target="tpu_custom_call" | custom-call | flops 3103784960 | bytes 8388608 | tf_op jit(solution)/shard_map/pallas_call | solution.py:345
  64.4 2.0 %copy.10 = f32[4,160,256]{2,1,0:T(8,128)} copy(f32[4,160,256]{2,1,0:T(8,128)} %shard_map.64) | data formatting | bytes 1310720

commit v5 on v4

--- a/solution.py
+++ b/solution.py
@@ -80,7 +80,7 @@
     beside, across, twin = e + 2 - 4 * x, lax.rem(e + 4, 8), e + 1 - 2 * c
     diagonal = lax.rem(beside + 4, 8)
     planes = (e, beside, across, diagonal)
-    others = [lax.rem(z + j, n) for j in range(1, n)]
+    others = [z + 1 - 2 * (z // 2), lax.rem(2 + 3 * z, 5), 3 - 3 * (z // 2)]
 
     def remote(src, dst, send, recv, elem, band):
         return pltpu.make_async_remote_copy(
@@ -216,8 +216,8 @@
         for copy in start_halo(part, z):
             copy.start()
 
-    def spread(part):
-        for s in others:
+    def spread(part, sources):
+        for s in sources:
             got(rows_of(start, part, s), a_r.at[part, s])
             for copy in start_halo(part, s):
                 copy.start()
@@ -266,24 +266,20 @@
             total = halo_slots(mid_lo, mid_hi, part, i)
             out[i, :, part * lanes:(part + 1) * lanes] = 2.0 * total - start[part, i]
 
-    def prepare_all():
-        ham_copy.wait()
-
-        def prepare(i, carry):
-            square = (basis, basis)
-            place = lax.broadcasted_iota(jnp.int32, square, 0)
-            scale = jnp.where(place < counts[i], 1.0 / jnp.full(square, width[0], F32), F32(0.0))
-            diagonal = jnp.where(place == lax.broadcasted_iota(jnp.int32, square, 1), center[0], F32(0.0))
-            for slot in range(SLOTS):
-                entries = ham_v[i, slot]
-                if slot == 0:
-                    entries = entries - diagonal
-                high, low = split(entries * scale)
-                ham_b[i, slot, :basis] = high
-                ham_b[i, slot, basis:] = low
-            return carry
-
-        lax.fori_loop(0, elements, prepare, 0)
+    def prepare(i):
+        square = (basis, basis)
+        place = lax.broadcasted_iota(jnp.int32, square, 0)
+        scale = jnp.where(place < counts[i], 1.0 / jnp.full(square, width[0], F32), F32(0.0))
+        diagonal_part = jnp.where(
+            place == lax.broadcasted_iota(jnp.int32, square, 1), center[0], F32(0.0)
+        )
+        for slot in range(SLOTS):
+            entries = ham_v[i, slot]
+            if slot == 0:
+                entries = entries - diagonal_part
+            high, low = split(entries * scale)
+            ham_b[i, slot, :basis] = high
+            ham_b[i, slot, basis:] = low
 
     send_own(0)
     send_own(1)
@@ -293,19 +289,24 @@
     orb_b[elements * rows:] = low
     rotate(0, z, True)
     gather_first(0)
+    ham_copy.wait()
+    prepare(0)
     gather_second(0)
+    prepare(1)
     gather_first(1)
     gather_third(0)
+    rotate(1, z, True)
+    rotated(0)
     gather_second(1)
-    rotated(0)
+    prepare(2)
     gather_third(1)
-    rotate(1, z, True)
+    prepare(3)
     rotated(1)
-    spread(0)
-    prepare_all()
+    spread(0, others)
     local_slots(start, 0)
-    spread(1)
+    spread(1, others[:1])
     middle(0)
+    spread(1, others[1:])
     local_slots(start, 1)
     middle(1)
     local_slots(mid, 0)

time: 67.3 us -> 69.8 us (1.037)
  the two profiles are of different devices: /device:TPU:0 before, /device:TPU:1 now
where the time goes in v5:
time: 69.8 us; the launch traced here: 69.6 us
  Pallas kernels  66.4 us (95%)
  local copies, waits for them, and re-layouts  1.98 us (3%)
  between operations  1.3 us (2%)
    pallas_call x1, Pallas kernels, shards(): pl.pallas_call(functools.partial(kernel, n), out_shape=jax.ShapeDtypeStru...  66.4 us
    unnamed x1, local copies, waits for them, and re-layouts  1.98 us

profile of v5, /device:TPU:1, one launch (start us, length us, event | category | flops | bytes accessed | tf_op | source)
XLA Modules:
  0.0 69.6 jit_solution(14368886249861440876)
XLA Ops:
  1.3 66.4 %shard_map.64 = f32[4,160,256]{2,1,0:T(8,128)} custom-call(f32[160,1024]{1,0:T(8,128)} %bitcast.1, f32[256,1024]{1,0:T(8,128)} %rot.1, s32[4]{0:T(128)} %counts.1, f32[1]{0:T(128)S(6)} %copy.8.center, f32[1]{0:T(128)S(6)} %copy.9.width, f32[4,7,160,160]{3,2,1,0:T(8,128)} %ham.1), custom_call_target="tpu_custom_call" | custom-call | flops 3103784960 | bytes 8388608 | tf_op jit(solution)/shard_map/pallas_call | solution.py:346
  67.7 2.0 %copy.10 = f32[4,160,256]{2,1,0:T(8,128)} copy(f32[4,160,256]{2,1,0:T(8,128)} %shard_map.64) | data formatting | bytes 1310720

commit v6 on v5

--- a/solution.py
+++ b/solution.py
@@ -65,8 +65,8 @@
 
 def kernel(
     n, orb, rot, counts, center, width, ham, out,
-    ham_v, ham_b, orb_v, orb_b, rot_b, res, acc_r, start, start_lo, start_hi, mid, mid_lo, mid_hi,
-    field, acc, ham_sem, orb_sem, rot_sem,
+    ham_v, ham_l, ham_h, orb_v, orb_b, rot_b, rot_s, res, start, start_lo, start_hi, mid, mid_lo, mid_hi,
+    field_l, field_h, acc, ham_sem, orb_sem, rot_sem,
     g_s, g_r, c_s, c_r, a_s, a_r, b_s, b_r, h_s, h_r,
 ):
     e, z = lax.axis_index("elem"), lax.axis_index("band")
@@ -191,64 +191,57 @@
             got(eighth(part, s, diagonal), g_r.at[3, part, s])
             over_core(part, s, 3).start()
 
-    def rotate(part, s, first):
-        columns = pl.ds(pl.multiple_of(s * depth, depth), depth)
-        high, low = split(rot_b[part, s])
-        both = jnp.dot(orb_b[:, columns], high, preferred_element_type=F32)
-        cross = jnp.dot(orb_b[:elements * rows, columns], low, preferred_element_type=F32)
-        total = both[:elements * rows] + both[elements * rows:] + cross
-        acc_r[part] = total if first else acc_r[part] + total
+    def halve(part, j):
+        high, low = split(rot_b[part, (z, *others)[j]])
+        rot_s[part, 0, j * depth:(j + 1) * depth] = high
+        rot_s[part, 1, j * depth:(j + 1) * depth] = low
 
     def rotated(part):
-        for s in others:
+        for j, s in enumerate(others):
             for k in range(4):
                 got(eighth(part, s, planes[k] + 1 - 2 * c), c_r.at[part, s, k])
-            rotate(part, s, False)
-        for i in range(elements):
-            place = lax.broadcasted_iota(jnp.int32, (rows, lanes), 0) + z * rows
-            alive = place < counts[i]
-            for b in range(n):
-                piece = acc_r[part, i * rows:(i + 1) * rows, b * lanes:(b + 1) * lanes]
-                res[part, b, i] = jnp.where(alive, piece, F32(0.0))
+            halve(part, j + 1)
+        for b in range(0, n, 2):
+            columns = slice(b * lanes, (b + 2) * lanes)
+            both = jnp.dot(orb_b[...], rot_s[part, 0, :, columns], preferred_element_type=F32)
+            cross = jnp.dot(orb_b[:elements * rows], rot_s[part, 1, :, columns], preferred_element_type=F32)
+            total = both[:elements * rows] + both[elements * rows:] + cross
+            for i in range(elements):
+                place = lax.broadcasted_iota(jnp.int32, (rows, 2 * lanes), 0) + z * rows
+                piece = jnp.where(place < counts[i], total[i * rows:(i + 1) * rows], F32(0.0))
+                res[part, b, i] = piece[:, :lanes]
+                res[part, b + 1, i] = piece[:, lanes:]
         for to in others:
             to_band(part, to).start()
         start[part, :, pl.ds(pl.multiple_of(z * rows, rows), rows)] = res[part, z]
         for copy in start_halo(part, z):
             copy.start()
 
-    def spread(part, sources):
-        for s in sources:
+    def spread(part):
+        for s in others:
             got(rows_of(start, part, s), a_r.at[part, s])
             for copy in start_halo(part, s):
                 copy.start()
 
-    def load(k, ref, part, i):
+    def load(ref, part, i, into, first):
         high, low = split(ref[part, i])
-        field[k, i, :, :lanes] = high
-        field[k, i, :, lanes:] = low
+        into[first:first + basis, :lanes] = high
+        into[first:first + basis, lanes:] = low
 
     def fold(r):
         return (r[:basis, :lanes] + r[:basis, lanes:]) + (r[basis:, :lanes] + r[basis:, lanes:])
 
     def local_slots(ref, part):
+        for i in range(-1, elements + 1):
+            load(ref, part, i % elements, field_l, (i + 1) * basis)
         for i in range(elements):
-            load(0, ref, part, i)
-
-        def body(i, carry):
-            r = jnp.dot(ham_b[i, 0], field[0, i], preferred_element_type=F32)
-            r += jnp.dot(ham_b[i, 1], field[0, lax.rem(i + elements - 1, elements)], preferred_element_type=F32)
-            r += jnp.dot(ham_b[i, 2], field[0, lax.rem(i + 1, elements)], preferred_element_type=F32)
-            acc[part, i] = fold(r)
-            return carry
-
-        lax.fori_loop(0, elements, body, 0)
+            around = field_l[i * basis:(i + 3) * basis]
+            acc[part, i] = fold(jnp.dot(ham_l[i], around, preferred_element_type=F32))
 
     def halo_slots(lo, hi, part, i):
-        load(1, lo, part, i)
-        load(2, hi, part, i)
-        r = jnp.dot(ham_b[i, 3], field[1, i], preferred_element_type=F32)
-        r += jnp.dot(ham_b[i, 4], field[2, i], preferred_element_type=F32)
-        return acc[part, i] + fold(r)
+        load(lo, part, i, field_h.at[i], 0)
+        load(hi, part, i, field_h.at[i], basis)
+        return acc[part, i] + fold(jnp.dot(ham_h[i], field_h[i], preferred_element_type=F32))
 
     def middle(part):
         for s in range(n):
@@ -273,40 +266,39 @@
         diagonal_part = jnp.where(
             place == lax.broadcasted_iota(jnp.int32, square, 1), center[0], F32(0.0)
         )
-        for slot in range(SLOTS):
-            entries = ham_v[i, slot]
-            if slot == 0:
-                entries = entries - diagonal_part
-            high, low = split(entries * scale)
-            ham_b[i, slot, :basis] = high
-            ham_b[i, slot, basis:] = low
+        own = (ham_v[i, 0] - diagonal_part) * scale
+        for into, blocks in (
+            (ham_l, [ham_v[i, 1] * scale, own, ham_v[i, 2] * scale]),
+            (ham_h, [ham_v[i, 3] * scale, ham_v[i, 4] * scale]),
+        ):
+            high, low = split(jnp.concatenate(blocks, axis=1))
+            into[i, :basis] = high
+            into[i, basis:] = low
 
     send_own(0)
     send_own(1)
     orb_copy.wait()
-    high, low = split(orb_v[...])
-    orb_b[:elements * rows] = high
-    orb_b[elements * rows:] = low
-    rotate(0, z, True)
+    for j, s in enumerate((z, *others)):
+        high, low = split(orb_v[:, pl.ds(pl.multiple_of(s * depth, depth), depth)])
+        orb_b[:elements * rows, j * depth:(j + 1) * depth] = high
+        orb_b[elements * rows:, j * depth:(j + 1) * depth] = low
+    halve(0, 0)
+    halve(1, 0)
     gather_first(0)
-    ham_copy.wait()
-    prepare(0)
     gather_second(0)
-    prepare(1)
     gather_first(1)
     gather_third(0)
-    rotate(1, z, True)
+    gather_second(1)
     rotated(0)
-    gather_second(1)
-    prepare(2)
     gather_third(1)
-    prepare(3)
     rotated(1)
-    spread(0, others)
+    spread(0)
+    ham_copy.wait()
+    for i in range(elements):
+        prepare(i)
     local_slots(start, 0)
-    spread(1, others[:1])
+    spread(1)
     middle(0)
-    spread(1, others[1:])
     local_slots(start, 1)
     middle(1)
     local_slots(mid, 0)
@@ -350,15 +342,17 @@
         out_specs=in_vmem,
         scratch_shapes=[
             pltpu.VMEM((elements, SLOTS, basis, basis), F32),
-            pltpu.VMEM((elements, SLOTS, 2 * basis, basis), BF16),
+            pltpu.VMEM((elements, 2 * basis, 3 * basis), BF16),
+            pltpu.VMEM((elements, 2 * basis, 2 * basis), BF16),
             pltpu.VMEM((elements * rows, bands), F32),
             pltpu.VMEM((2 * elements * rows, bands), BF16),
             pltpu.VMEM((PARTS, n, depth, n * lanes), F32),
+            pltpu.VMEM((PARTS, 2, bands, n * lanes), BF16),
             pltpu.VMEM((PARTS, n, elements, rows, lanes), F32),
-            pltpu.VMEM((PARTS, elements * rows, n * lanes), F32),
             pltpu.VMEM(own, F32), pltpu.VMEM(own, F32), pltpu.VMEM(own, F32),
             pltpu.VMEM(own, F32), pltpu.VMEM(own, F32), pltpu.VMEM(own, F32),
-            pltpu.VMEM((3, elements, basis, 2 * lanes), BF16),
+            pltpu.VMEM(((elements + 2) * basis, 2 * lanes), BF16),
+            pltpu.VMEM((elements, 2 * basis, 2 * lanes), BF16),
             pltpu.VMEM(own, F32),
             dma(()), dma(()), dma((PARTS, n)),
             dma((4, PARTS, n)), dma((4, PARTS, n)),

time: 69.8 us -> 67.6 us (0.968)
  the two profiles are of different devices: /device:TPU:1 before, /device:TPU:0 now
where the time goes in v6:
time: 67.6 us; the launch traced here: 67 us
  Pallas kernels  63.7 us (94%)
  local copies, waits for them, and re-layouts  1.98 us (3%)
  between operations  1.3 us (2%)
    pallas_call x1, Pallas kernels, shards(): pl.pallas_call(functools.partial(kernel, n), out_shape=jax.ShapeDtypeStru...  63.7 us
    unnamed x1, local copies, waits for them, and re-layouts  1.98 us

profile of v6, /device:TPU:0, one launch (start us, length us, event | category | flops | bytes accessed | tf_op | source)
XLA Modules:
  0.0 67.0 jit_solution(13667970058983986277)
XLA Ops:
  1.3 63.7 %shard_map.64 = f32[4,160,256]{2,1,0:T(8,128)} custom-call(f32[160,1024]{1,0:T(8,128)} %bitcast.1, f32[256,1024]{1,0:T(8,128)} %rot.1, s32[4]{0:T(128)} %counts.1, f32[1]{0:T(128)S(6)} %copy.8.center, f32[1]{0:T(128)S(6)} %copy.9.width, f32[4,7,160,160]{3,2,1,0:T(8,128)} %ham.1), custom_call_target="tpu_custom_call" | custom-call | flops 3103784960 | bytes 8388608 | tf_op jit(solution)/shard_map/pallas_call | solution.py:338
  65.0 2.0 %copy.10 = f32[4,160,256]{2,1,0:T(8,128)} copy(f32[4,160,256]{2,1,0:T(8,128)} %shard_map.64) | data formatting | bytes 1310720

commit v7 on v6

--- a/solution.py
+++ b/solution.py
@@ -276,15 +276,15 @@
             into[i, basis:] = low
 
     send_own(0)
-    send_own(1)
     orb_copy.wait()
     for j, s in enumerate((z, *others)):
         high, low = split(orb_v[:, pl.ds(pl.multiple_of(s * depth, depth), depth)])
         orb_b[:elements * rows, j * depth:(j + 1) * depth] = high
         orb_b[elements * rows:, j * depth:(j + 1) * depth] = low
     halve(0, 0)
+    gather_first(0)
+    send_own(1)
     halve(1, 0)
-    gather_first(0)
     gather_second(0)
     gather_first(1)
     gather_third(0)

time: 67.6 us -> 65 us (0.962)
  Pallas kernels: 63.7 us -> 61.2 us
    pallas_call x1, Pallas kernels: 63.7 us -> 61.2 us  [shards(): pl.pallas_call(functools.partial(kernel, n), out_shape=jax.ShapeDtypeStru...]
where the time goes in v7:
time: 65 us; the launch traced here: 64.4 us
  Pallas kernels  61.2 us (94%)
  local copies, waits for them, and re-layouts  1.98 us (3%)
  between operations  1.3 us (2%)
    pallas_call x1, Pallas kernels, shards(): pl.pallas_call(functools.partial(kernel, n), out_shape=jax.ShapeDtypeStru...  61.2 us
    unnamed x1, local copies, waits for them, and re-layouts  1.98 us

profile of v7, /device:TPU:0, one launch (start us, length us, event | category | flops | bytes accessed | tf_op | source)
XLA Modules:
  0.0 64.4 jit_solution(7988058382811427251)
XLA Ops:
  1.3 61.2 %shard_map.64 = f32[4,160,256]{2,1,0:T(8,128)} custom-call(f32[160,1024]{1,0:T(8,128)} %bitcast.1, f32[256,1024]{1,0:T(8,128)} %rot.1, s32[4]{0:T(128)} %counts.1, f32[1]{0:T(128)S(6)} %copy.8.center, f32[1]{0:T(128)S(6)} %copy.9.width, f32[4,7,160,160]{3,2,1,0:T(8,128)} %ham.1), custom_call_target="tpu_custom_call" | custom-call | flops 3103784960 | bytes 8388608 | tf_op jit(solution)/shard_map/pallas_call | solution.py:338
  62.5 2.0 %copy.10 = f32[4,160,256]{2,1,0:T(8,128)} copy(f32[4,160,256]{2,1,0:T(8,128)} %shard_map.64) | data formatting | bytes 1310720

commit v8 on v7

--- a/solution.py
+++ b/solution.py
@@ -217,8 +217,8 @@
         for copy in start_halo(part, z):
             copy.start()
 
-    def spread(part):
-        for s in others:
+    def spread(part, sources):
+        for s in sources:
             got(rows_of(start, part, s), a_r.at[part, s])
             for copy in start_halo(part, s):
                 copy.start()
@@ -285,20 +285,23 @@
     gather_first(0)
     send_own(1)
     halve(1, 0)
+    ham_copy.wait()
+    prepare(0)
     gather_second(0)
+    prepare(1)
+    gather_third(0)
+    prepare(2)
     gather_first(1)
-    gather_third(0)
+    rotated(0)
     gather_second(1)
-    rotated(0)
+    prepare(3)
     gather_third(1)
     rotated(1)
-    spread(0)
-    ham_copy.wait()
-    for i in range(elements):
-        prepare(i)
+    spread(0, others)
     local_slots(start, 0)
-    spread(1)
+    spread(1, others[:1])
     middle(0)
+    spread(1, others[1:])
     local_slots(start, 1)
     middle(1)
     local_slots(mid, 0)

time: 65 us -> 71.3 us (1.097)
  Pallas kernels: 61.2 us -> 67.8 us
    pallas_call x1, Pallas kernels: 61.2 us -> 67.8 us  [shards(): pl.pallas_call(functools.partial(kernel, n), out_shape=jax.ShapeDtypeStru...]
where the time goes in v8:
time: 71.3 us; the launch traced here: 71.1 us
  Pallas kernels  67.8 us (95%)
  local copies, waits for them, and re-layouts  1.98 us (3%)
  between operations  1.3 us (2%)
    pallas_call x1, Pallas kernels, shards(): pl.pallas_call(functools.partial(kernel, n), out_shape=jax.ShapeDtypeStru...  67.8 us
    unnamed x1, local copies, waits for them, and re-layouts  1.98 us

profile of v8, /device:TPU:0, one launch (start us, length us, event | category | flops | bytes accessed | tf_op | source)
XLA Modules:
  0.0 71.1 jit_solution(17993706745165447846)
XLA Ops:
  1.3 67.8 %shard_map.64 = f32[4,160,256]{2,1,0:T(8,128)} custom-call(f32[160,1024]{1,0:T(8,128)} %bitcast.1, f32[256,1024]{1,0:T(8,128)} %rot.1, s32[4]{0:T(128)} %counts.1, f32[1]{0:T(128)S(6)} %copy.8.center, f32[1]{0:T(128)S(6)} %copy.9.width, f32[4,7,160,160]{3,2,1,0:T(8,128)} %ham.1), custom_call_target="tpu_custom_call" | custom-call | flops 3103784960 | bytes 8388608 | tf_op jit(solution)/shard_map/pallas_call | solution.py:341
  69.1 2.0 %copy.10 = f32[4,160,256]{2,1,0:T(8,128)} copy(f32[4,160,256]{2,1,0:T(8,128)} %shard_map.64) | data formatting | bytes 1310720

commit v9 on v8

--- a/solution.py
+++ b/solution.py
@@ -285,23 +285,23 @@
     gather_first(0)
     send_own(1)
     halve(1, 0)
-    ham_copy.wait()
-    prepare(0)
     gather_second(0)
-    prepare(1)
     gather_third(0)
-    prepare(2)
     gather_first(1)
+    gather_second(1)
     rotated(0)
-    gather_second(1)
-    prepare(3)
     gather_third(1)
     rotated(1)
     spread(0, others)
+    ham_copy.wait()
+    prepare(0)
+    prepare(1)
+    spread(1, others[:1])
+    prepare(2)
+    prepare(3)
+    spread(1, others[1:])
     local_slots(start, 0)
-    spread(1, others[:1])
     middle(0)
-    spread(1, others[1:])
     local_slots(start, 1)
     middle(1)
     local_slots(mid, 0)

time: 71.3 us -> 69.1 us (0.969)
  Pallas kernels: 67.8 us -> 65.6 us
    pallas_call x1, Pallas kernels: 67.8 us -> 65.6 us  [shards(): pl.pallas_call(functools.partial(kernel, n), out_shape=jax.ShapeDtypeStru...]
where the time goes in v9:
time: 69.1 us; the launch traced here: 68.9 us
  Pallas kernels  65.6 us (95%)
  local copies, waits for them, and re-layouts  1.98 us (3%)
  between operations  1.3 us (2%)
    pallas_call x1, Pallas kernels, shards(): pl.pallas_call(functools.partial(kernel, n), out_shape=jax.ShapeDtypeStru...  65.6 us
    unnamed x1, local copies, waits for them, and re-layouts  1.98 us

profile of v9, /device:TPU:0, one launch (start us, length us, event | category | flops | bytes accessed | tf_op | source)
XLA Modules:
  0.0 68.9 jit_solution(11174952275053496479)
XLA Ops:
  1.3 65.6 %shard_map.64 = f32[4,160,256]{2,1,0:T(8,128)} custom-call(f32[160,1024]{1,0:T(8,128)} %bitcast.1, f32[256,1024]{1,0:T(8,128)} %rot.1, s32[4]{0:T(128)} %counts.1, f32[1]{0:T(128)S(6)} %copy.8.center, f32[1]{0:T(128)S(6)} %copy.9.width, f32[4,7,160,160]{3,2,1,0:T(8,128)} %ham.1), custom_call_target="tpu_custom_call" | custom-call | flops 3103784960 | bytes 8388608 | tf_op jit(solution)/shard_map/pallas_call | solution.py:341
  66.9 2.0 %copy.10 = f32[4,160,256]{2,1,0:T(8,128)} copy(f32[4,160,256]{2,1,0:T(8,128)} %shard_map.64) | data formatting | bytes 1310720

commit v10 on v7

--- a/solution.py
+++ b/solution.py
@@ -196,6 +196,10 @@
         rot_s[part, 0, j * depth:(j + 1) * depth] = high
         rot_s[part, 1, j * depth:(j + 1) * depth] = low
 
+    def exchange(part):
+        for to in others:
+            to_band(part, to).start()
+
     def rotated(part):
         for j, s in enumerate(others):
             for k in range(4):
@@ -211,8 +215,8 @@
                 piece = jnp.where(place < counts[i], total[i * rows:(i + 1) * rows], F32(0.0))
                 res[part, b, i] = piece[:, :lanes]
                 res[part, b + 1, i] = piece[:, lanes:]
-        for to in others:
-            to_band(part, to).start()
+        if part == 0:
+            exchange(part)
         start[part, :, pl.ds(pl.multiple_of(z * rows, rows), rows)] = res[part, z]
         for copy in start_halo(part, z):
             copy.start()
@@ -293,6 +297,7 @@
     gather_third(1)
     rotated(1)
     spread(0)
+    exchange(1)
     ham_copy.wait()
     for i in range(elements):
         prepare(i)

time: 65 us -> 64.5 us (level)
  no operation moved by 1% of the time
where the time goes in v10:
time: 64.5 us; the launch traced here: 64.2 us
  Pallas kernels  60.9 us (94%)
  local copies, waits for them, and re-layouts  1.98 us (3%)
  between operations  1.3 us (2%)
    pallas_call x1, Pallas kernels, shards(): pl.pallas_call(functools.partial(kernel, n), out_shape=jax.ShapeDtypeStru...  60.9 us
    unnamed x1, local copies, waits for them, and re-layouts  1.98 us

profile of v10, /device:TPU:0, one launch (start us, length us, event | category | flops | bytes accessed | tf_op | source)
XLA Modules:
  0.0 64.2 jit_solution(18012972480654693386)
XLA Ops:
  1.3 60.9 %shard_map.64 = f32[4,160,256]{2,1,0:T(8,128)} custom-call(f32[160,1024]{1,0:T(8,128)} %bitcast.1, f32[256,1024]{1,0:T(8,128)} %rot.1, s32[4]{0:T(128)} %counts.1, f32[1]{0:T(128)S(6)} %copy.8.center, f32[1]{0:T(128)S(6)} %copy.9.width, f32[4,7,160,160]{3,2,1,0:T(8,128)} %ham.1), custom_call_target="tpu_custom_call" | custom-call | flops 3103784960 | bytes 8388608 | tf_op jit(solution)/shard_map/pallas_call | solution.py:343
  62.2 2.0 %copy.10 = f32[4,160,256]{2,1,0:T(8,128)} copy(f32[4,160,256]{2,1,0:T(8,128)} %shard_map.64) | data formatting | bytes 1310720
